TPU v7x, 128 devices: a whole 4x4x4 slice. The times are simulated.
128 devices in a mesh: coef: 8 (over x, y_hi), obs: 16 (over z, y_lo, core).
Axes of the slice: x: 4, y: 4 (y_hi: 2, y_lo: 2; y = y_hi * 2 + y_lo), z: 4, core: 2. Of those that a mesh axis runs over, the one named last changes fastest.
Arguments:
- sample_index: int32 [16384], P('obs'), may hold values from 0 to 16383
- colatitude: float32 [16384], replicated, may hold values from 0.12 to 3.02
- longitude: float32 [16384], replicated, may hold values from -3.140625 to 3.140625
- orders: int32 [128], P('coef'), may hold values from 1 to 237
- observed: float32 [16384], P('obs'), may hold values from -6 to 6
- whitening: bfloat16 [16384, 1024], P('obs')
Outputs:
- normal: float32 [8192, 8192], P(('coef', 'obs'))
- rhs: float32 [8192], P('coef')
Inputs may be any that keep to these rules, and one draw needn't show every extreme that they name: `orders`: so every degree m + l stays at most 300.
All inputs are finite; a program needn't handle non-finite values.
Results may differ from a plain program's by a relative error of at most 0.019.
Values may be sent and summed in bfloat16 or wider, within the bound.
A program may use at most 128 MiB of HBM per device.

v0:
```python
import jax
import jax.numpy as jnp
from jax import lax
from jax.sharding import PartitionSpec as P

LEV = 64
NMAX = 300


def shifted(block, axis, distance):
    devices = range(lax.axis_size(axis))
    route = [((i - distance) % len(devices), i) for i in devices]
    return lax.ppermute(block, axis, route)


def legendre_block(colat_rows, long_rows, orders, parity):
    order_val = orders.astype(jnp.float32)[:, None]
    counter = jnp.arange(1, NMAX + 1, dtype=jnp.float32)[None, :]
    log_const = jnp.sum(
        jnp.where(
            counter <= order_val, 0.5 * jnp.log((2.0 * counter + 1.0) / (2.0 * counter)), 0.0
        ),
        axis=1,
        keepdims=True,
    )
    sectorial = jnp.sqrt(jnp.float32(2.0)) * jnp.exp(
        log_const + order_val * jnp.log(jnp.sin(colat_rows))[None, :]
    )
    cosine = jnp.cos(colat_rows)[None, :]

    def level(carry, degree_step):
        lower, lowest = carry
        degree = order_val + degree_step
        rise_term = jnp.sqrt(
            (2.0 * degree - 1.0)
            * (2.0 * degree + 1.0)
            / ((degree - order_val) * (degree + order_val))
        )
        fall_term = jnp.sqrt(
            (2.0 * degree + 1.0)
            * (degree + order_val - 1.0)
            * (degree - order_val - 1.0)
            / ((2.0 * degree - 3.0) * (degree + order_val) * (degree - order_val))
        )
        value = rise_term * cosine * lower - fall_term * lowest
        return ((value, lower), value)

    _, higher = lax.scan(
        level, (sectorial, jnp.zeros_like(sectorial)), jnp.arange(1, LEV, dtype=jnp.float32)
    )
    levels = jnp.concatenate([sectorial[None], higher], axis=0)
    phase_arg = order_val * long_rows[None, :]
    harmonic = jnp.where(parity[:, None] == 0, jnp.cos(phase_arg), jnp.sin(phase_arg))
    result = jnp.transpose(levels, (1, 0, 2)) * harmonic[:, None, :]
    return result.reshape(orders.shape[0] * LEV, colat_rows.shape[0])


def pair_product(left, right):
    return lax.dot_general(
        left, right, (((1,), (1,)), ((), ())), preferred_element_type=jnp.float32
    )


def forward_step(block):
    return shifted(block, "coef", 1)


def on_device(sample_index, colatitude, longitude, orders, observed, whitening):
    coef_count = lax.axis_size("coef")
    obs_count = lax.axis_size("obs")
    block_pos = lax.axis_index("coef")
    slot_count = orders.shape[0]
    row_count = sample_index.shape[0]
    parity = (block_pos * slot_count + jnp.arange(slot_count, dtype=jnp.int32)) % 2
    colat_rows = colatitude[sample_index]
    long_rows = longitude[sample_index]
    design = legendre_block(colat_rows, long_rows, orders, parity).astype(jnp.bfloat16)
    filtered = pair_product(design, whitening).astype(jnp.bfloat16)
    whitened = jnp.dot(whitening.astype(jnp.float32), observed, precision=lax.Precision.HIGHEST)
    rhs_part = jnp.dot(filtered.astype(jnp.float32), whitened, precision=lax.Precision.HIGHEST)
    total_rows = row_count * obs_count
    rhs_total = lax.psum(rhs_part, "obs") / jnp.sqrt(jnp.float32(total_rows))
    inv_rows = 1.0 / total_rows
    block_cols = filtered.shape[0]
    all_cols = block_cols * coef_count
    row_share = block_cols // obs_count

    def make_tile(other):
        return pair_product(filtered, other) * inv_rows

    tiles = [make_tile(filtered)]
    places = [block_pos]
    moving = filtered
    for offset_step in range(1, coef_count):
        moving = forward_step(moving)
        tiles.append(make_tile(moving))
        places.append((block_pos - offset_step) % coef_count)
    stacked = jnp.concatenate(tiles, axis=1)
    reduced = lax.psum_scatter(
        stacked.astype(jnp.bfloat16), "obs", scatter_dimension=0, tiled=True
    ).astype(jnp.float32)
    tiles = [reduced[:, pos * block_cols : (pos + 1) * block_cols] for pos in range(len(tiles))]
    normal = jnp.zeros((row_share, all_cols), jnp.float32)
    for tile_rows, column_block in zip(tiles, places):
        normal = lax.dynamic_update_slice(
            normal, tile_rows, (jnp.int32(0), column_block * block_cols)
        )
    return (normal, rhs_total)


def solution(mesh):
    placed = (P("obs"), P(), P(), P("coef"), P("obs"), P("obs", None))
    return jax.shard_map(
        on_device,
        mesh=mesh,
        in_specs=placed,
        out_specs=(P(("coef", "obs"), None), P("coef")),
        check_vma=False,
    )
```

profile of v0, /device:TPU:1, one launch (start us, length us, event | category | flops | bytes accessed | tf_op | source)
XLA Modules:
  0.0 814.8 jit_solution(530090162565812021)
XLA Ops:
  8.8 5.9 gather_fusion
  14.7 6.2 gather_fusion.1
  21.5 217.0 %while.17 = (s32[]{:T(128)}, f32[16,1024]{1,0:T(8,128)S(1)}, f32[16,1024]{1,0:T(8,128)S(1)}, f32[63,16,1024]{2,0,1:T(8,128)}, f32[16,1]{0,1:T(1,128)S(1)}, /*ind...) while((s32[]{:T(128)}, f32[16,1024]{1,0:T(8,128)S(1)}, f32[16,1024]{1,0:T(8,128)S(1)}, ...), condition=%wide.region_2.3_spmd, body=%wide.region_1.2_spmd.sunk | while | flops 65810 | bytes 725425 | solution.py:48
  238.6 2.9 fusion.2
  243.9 3.8 collective-permute-start
  247.7 47.4 %collective-permute-done = bf16[1024,1024]{1,0:T(8,128)(2,1)S(1)} collective-permute-done((bf16[1024,1024]{1,0:T(8,128)(2,1)S(1)}, bf16[1024,1024]{1,0:T(8,128)(2,1)S(1)}, u32[]{:S(2)}, u32[]{:S(2)}) %collective-permute-start) | collective-permute-done | bytes 2097184 | tf_op jit(solution)/shard_map/ppermute | solution.py:13
  295.7 48.7 %collective-permute-done.1 = bf16[1024,1024]{1,0:T(8,128)(2,1)S(1)} collective-permute-done((bf16[1024,1024]{1,0:T(8,128)(2,1)S(1)}, bf16[1024,1024]{1,0:T(8,128)(2,1)S(1)}, u32[]{:S(2)}, u32[]{:S(2)}) %collective-permute-start.1) | collective-permute-done | bytes 2097184 | tf_op jit(solution)/shard_map/ppermute | solution.py:13
  344.4 48.4 %collective-permute-done.2 = bf16[1024,1024]{1,0:T(8,128)(2,1)S(1)} collective-permute-done((bf16[1024,1024]{1,0:T(8,128)(2,1)S(1)}, bf16[1024,1024]{1,0:T(8,128)(2,1)S(1)}, u32[]{:S(2)}, u32[]{:S(2)}) %collective-permute-start.2) | collective-permute-done | bytes 2097184 | tf_op jit(solution)/shard_map/ppermute | solution.py:13
  392.8 47.5 %collective-permute-done.3 = bf16[1024,1024]{1,0:T(8,128)(2,1)S(1)} collective-permute-done((bf16[1024,1024]{1,0:T(8,128)(2,1)S(1)}, bf16[1024,1024]{1,0:T(8,128)(2,1)S(1)}, u32[]{:S(2)}, u32[]{:S(2)}) %collective-permute-start.3) | collective-permute-done | bytes 2097184 | tf_op jit(solution)/shard_map/ppermute | solution.py:13
  440.2 46.6 %collective-permute-done.4 = bf16[1024,1024]{1,0:T(8,128)(2,1)S(1)} collective-permute-done((bf16[1024,1024]{1,0:T(8,128)(2,1)S(1)}, bf16[1024,1024]{1,0:T(8,128)(2,1)S(1)}, u32[]{:S(2)}, u32[]{:S(2)}) %collective-permute-start.4) | collective-permute-done | bytes 2097184 | tf_op jit(solution)/shard_map/ppermute | solution.py:13
  486.8 3.7 fusion.3
  490.5 3.8 fusion.4
  494.3 3.7 fusion.5
  498.0 34.4 %collective-permute-done.5 = bf16[1024,1024]{1,0:T(8,128)(2,1)S(1)} collective-permute-done((bf16[1024,1024]{1,0:T(8,128)(2,1)S(1)}, bf16[1024,1024]{1,0:T(8,128)(2,1)S(1)}, u32[]{:S(2)}, u32[]{:S(2)}) %collective-permute-start.5) | collective-permute-done | bytes 2097184 | tf_op jit(solution)/shard_map/ppermute | solution.py:13
  532.4 3.7 fusion.6
  536.2 3.8 fusion.7
  539.9 3.7 fusion.8
  543.7 3.7 fusion.9
  547.4 29.8 %collective-permute-done.6 = bf16[1024,1024]{1,0:T(8,128)(2,1)S(1)} collective-permute-done((bf16[1024,1024]{1,0:T(8,128)(2,1)S(1)}, bf16[1024,1024]{1,0:T(8,128)(2,1)S(1)}, u32[]{:S(2)}, u32[]{:S(2)}) %collective-permute-start.6) | collective-permute-done | bytes 2097184 | tf_op jit(solution)/shard_map/ppermute | solution.py:13
  577.2 3.7 fusion.10
  580.8 21.3 %copy.53 = bf16[1024,8192]{1,0:T(8,128)(2,1)} copy(bf16[1024,8192]{0,1:T(8,128)(2,1)} %fusion.10) | data formatting | bytes 33554432
  606.3 35.0 %psum.7 = f32[1024]{0:T(1024)S(1)} all-reduce(f32[1024]{0:T(1024)S(1)} %bitcast.65), channel_id=1, replica_groups=mesh['coef'=8,'obs'=16] {'obs'}, use_global_device_ids=true, to_apply=%region_4.5 | all-reduce | flops 1024 | bytes 8192 | tf_op jit(solution)/shard_map/psum | solution.py:82
  641.9 145.4 %reduce-scatter.4.cloned.1.call-done = bf16[64,8192]{1,0:T(8,128)(2,1)} async-done(((bf16[1024,8192]{1,0:T(8,128)(2,1)}), bf16[64,8192]{1,0:T(8,128)(2,1)}) %reduce-scatter.4.cloned.1.call-update) | async-done | bytes 1048592
  790.0 3.2 fusion.17
  (507 shorter events, 241.8 us)
Async XLA Ops:
  7.2 234.3 %copy-start = (bf16[1024,1024]{1,0:T(8,128)(2,1)S(1)}, bf16[1024,1024]{1,0:T(8,128)(2,1)}, u32[]{:S(2)}) copy-start(bf16[1024,1024]{1,0:T(8,128)(2,1)} %param.13) | copy-start | bytes 6291460
  7.2 780.1 %reduce-scatter.4.cloned.1.call-start = ((), (), s32[]{:S(2)}) async-start(), calls=%async_computation.1 | async-start | bytes 17825792
  8.8 6.0 copy-start.1
  243.9 333.3 %copy-start.3 = (bf16[1024,1024]{1,0:T(8,128)(2,1)}, bf16[1024,1024]{1,0:T(8,128)(2,1)S(1)}, u32[]{:S(2)}) copy-start(bf16[1024,1024]{1,0:T(8,128)(2,1)S(1)} %convolution_convert_fusion) | copy-start | bytes 6291460
  243.9 51.2 %collective-permute-start = (bf16[1024,1024]{1,0:T(8,128)(2,1)S(1)}, bf16[1024,1024]{1,0:T(8,128)(2,1)S(1)}, u32[]{:S(2)}, u32[]{:S(2)}) collective-permute-start(bf16[1024,1024]{1,0:T(8,128)(2,1)S(1)} %convolution_convert_fusion), channel_id=1, source_target_pairs={{112,0},{0,16},{16,32},{32,48},{48,64},{64,80},{80,96},{96,112},{1... | collective-permute-start | bytes 6291464 | tf_op jit(solution)/shard_map/ppermute | solution.py:13
  295.0 49.3 %collective-permute-start.1 = (bf16[1024,1024]{1,0:T(8,128)(2,1)S(1)}, bf16[1024,1024]{1,0:T(8,128)(2,1)S(1)}, u32[]{:S(2)}, u32[]{:S(2)}) collective-permute-start(bf16[1024,1024]{1,0:T(8,128)(2,1)S(1)} %collective-permute-done), channel_id=1, source_target_pairs={{112,0},{0,16},{16,32},{32,48},{48,64},{64,80},{80,96},{96,112},{1... | collective-permute-start | bytes 6291464 | tf_op jit(solution)/shard_map/ppermute | solution.py:13
  344.4 48.4 %collective-permute-start.2 = (bf16[1024,1024]{1,0:T(8,128)(2,1)S(1)}, bf16[1024,1024]{1,0:T(8,128)(2,1)S(1)}, u32[]{:S(2)}, u32[]{:S(2)}) collective-permute-start(bf16[1024,1024]{1,0:T(8,128)(2,1)S(1)} %collective-permute-done.1), channel_id=1, source_target_pairs={{112,0},{0,16},{16,32},{32,48},{48,64},{64,80},{80,96},{96,112},{1... | collective-permute-start | bytes 6291464 | tf_op jit(solution)/shard_map/ppermute | solution.py:13
  392.8 47.5 %collective-permute-start.3 = (bf16[1024,1024]{1,0:T(8,128)(2,1)S(1)}, bf16[1024,1024]{1,0:T(8,128)(2,1)S(1)}, u32[]{:S(2)}, u32[]{:S(2)}) collective-permute-start(bf16[1024,1024]{1,0:T(8,128)(2,1)S(1)} %collective-permute-done.2), channel_id=1, source_target_pairs={{112,0},{0,16},{16,32},{32,48},{48,64},{64,80},{80,96},{96,112},{1... | collective-permute-start | bytes 6291464 | tf_op jit(solution)/shard_map/ppermute | solution.py:13
  440.2 46.6 %collective-permute-start.4 = (bf16[1024,1024]{1,0:T(8,128)(2,1)S(1)}, bf16[1024,1024]{1,0:T(8,128)(2,1)S(1)}, u32[]{:S(2)}, u32[]{:S(2)}) collective-permute-start(bf16[1024,1024]{1,0:T(8,128)(2,1)S(1)} %collective-permute-done.3), channel_id=1, source_target_pairs={{112,0},{0,16},{16,32},{32,48},{48,64},{64,80},{80,96},{96,112},{1... | collective-permute-start | bytes 6291464 | tf_op jit(solution)/shard_map/ppermute | solution.py:13
  486.8 45.6 %collective-permute-start.5 = (bf16[1024,1024]{1,0:T(8,128)(2,1)S(1)}, bf16[1024,1024]{1,0:T(8,128)(2,1)S(1)}, u32[]{:S(2)}, u32[]{:S(2)}) collective-permute-start(bf16[1024,1024]{1,0:T(8,128)(2,1)S(1)} %collective-permute-done.4), channel_id=1, source_target_pairs={{112,0},{0,16},{16,32},{32,48},{48,64},{64,80},{80,96},{96,112},{1... | collective-permute-start | bytes 6291464 | tf_op jit(solution)/shard_map/ppermute | solution.py:13
  532.4 44.7 %collective-permute-start.6 = (bf16[1024,1024]{1,0:T(8,128)(2,1)S(1)}, bf16[1024,1024]{1,0:T(8,128)(2,1)S(1)}, u32[]{:S(2)}, u32[]{:S(2)}) collective-permute-start(bf16[1024,1024]{1,0:T(8,128)(2,1)S(1)} %collective-permute-done.5), channel_id=1, source_target_pairs={{112,0},{0,16},{16,32},{32,48},{48,64},{64,80},{80,96},{96,112},{1... | collective-permute-start | bytes 6291464 | tf_op jit(solution)/shard_map/ppermute | solution.py:13
  602.1 0.7 copy-start.11
  602.3 2.2 copy-start.4
  805.2 1.0 copy-start.10
  805.2 1.0 copy-start.9
  805.2 1.1 copy-start.8
  805.2 1.2 copy-start.7
  805.2 1.2 copy-start.6
  805.2 1.3 copy-start.5
  806.6 1.3 copy-start.2
Sparse Core Ops, SparseCore 0:
  602.3 184.9 reduce-scatter.3
where the time goes:
time: 819 us; the launch traced here: 815 us
  waiting for transfers between devices  448 us (55%)
  local copies, waits for them, and re-layouts  222 us (27%)
  other arithmetic  52.4 us (6%)
  matrix products  35.7 us (4%)
  blocking collectives  35 us (4%)
  between operations  14.5 us (2%)
    ppermute x7, waiting for transfers between devices, shifted(): return lax.ppermute(block, axis, route)  303 us
    unnamed x2, waiting for transfers between devices  145 us
    dynamic_update_slice x126, local copies, waits for them, and re-layouts, legendre_block(): lax.scan(level, (sectorial, jnp.zeros_like(sectorial)), jnp.arange(1, LEV...  130 us
    sqrt x63, other arithmetic, level(): jnp.sqrt((2.0 * degree - 1.0) * (2.0 * degree + 1.0) / ((degree - order_v...  41.7 us
    dynamic_slice x63, local copies, waits for them, and re-layouts, legendre_block(): lax.scan(level, (sectorial, jnp.zeros_like(sectorial)), jnp.arange(1, LEV...  36.9 us
    psum x1, blocking collectives, on_device(): rhs_total = lax.psum(rhs_part, 'obs') / jnp.sqrt(jnp.float32(total_rows))  35 us
    dot_general x9, matrix products, pair_product(): lax.dot_general(left, right, (((1,), (1,)), ((), ())), preferred_element_...  32.2 us
    unnamed x26, local copies, waits for them, and re-layouts  26.9 us
  transfers between devices with their start and end apart: 8, of which 8 were waited for; matrix products, arithmetic and copies ran while one was open for 4% of the time, Pallas kernels for 0%

commit v1 on v0

v1 whole, which is shorter than its diff:
```python
import functools
import math

import jax
import jax.numpy as jnp
from jax import lax
from jax.experimental import pallas as pl
from jax.experimental.pallas import tpu as pltpu
from jax.sharding import PartitionSpec as P

LEV = 64
NMAX = 300
SEG = 1024
SET = 512
NSETS = 16
NEAR = 9
MIRROR = 7
TILE = 256
PITCH = 65
F32 = jnp.float32
BF16 = jnp.bfloat16
MESH = pl.DeviceIdType.MESH
NT = (((1,), (1,)), ((), ()))
COS_TERMS = [(-1.0) ** i * (2.0 * math.pi) ** (2 * i) / math.factorial(2 * i) for i in range(11)]


def prep_kernel(index_ref, colat_ref, long_ref, orders_ref, observed_ref, rows_ref, table_ref):
    index = index_ref[...]
    high, low = index // 128, index % 128
    pos = lax.broadcasted_iota(jnp.int32, (128, SEG), 0)
    pick_high = (pos == high).astype(F32)
    pick_low = (pos == low).astype(F32)

    def look_up(table):
        found = lax.dot_general(
            table, pick_high, (((0,), (0,)), ((), ())),
            precision=lax.Precision.HIGHEST, preferred_element_type=F32,
        )
        return jnp.sum(found * pick_low, axis=0, keepdims=True)

    colat = look_up(colat_ref[...])
    longitude = look_up(long_ref[...])
    rows_ref[...] = jnp.zeros(rows_ref.shape, F32)
    rows_ref[0:1, :] = jnp.log(jnp.sin(colat))
    rows_ref[1:2, :] = jnp.cos(colat)
    rows_ref[2:3, :] = longitude * (0.5 / math.pi)
    rows_ref[3:4, :] = observed_ref[...]

    order = orders_ref[...].astype(F32)
    counter = (lax.broadcasted_iota(jnp.int32, (16, 384), 1) + 1).astype(F32)
    log_const = jnp.sum(
        jnp.where(counter <= order, 0.5 * jnp.log((2.0 * counter + 1.0) / (2.0 * counter)), 0.0),
        axis=1, keepdims=True,
    )
    lane = lax.broadcasted_iota(jnp.int32, (16, 128), 1)
    step = jnp.maximum(lane % 64, 1).astype(F32)
    degree = order + step
    rise = jnp.sqrt((2.0 * degree - 1.0) * (2.0 * degree + 1.0) / (step * (degree + order)))
    fall = jnp.sqrt(
        (2.0 * degree + 1.0) * (degree + order - 1.0) * (step - 1.0)
        / ((2.0 * degree - 3.0) * (degree + order) * step)
    )
    table = jnp.where(lane < 64, rise, fall)
    table = jnp.where(lane == 0, order, table)
    table_ref[...] = jnp.where(lane == 64, log_const, table)


def split_rows(row):
    high = row.astype(BF16).astype(F32)
    rest = row - high
    middle = rest.astype(BF16).astype(F32)
    low = rest - middle
    place = lax.broadcasted_iota(jnp.int32, (16, row.shape[1]), 0)
    pieces = jnp.where(place == 0, high, jnp.where(place == 1, middle, jnp.where(place == 2, low, 0.0)))
    return pieces.astype(BF16)


def main_kernel(
    rows_ref, table_ref, white_ref, out_ref, rhs_ref,
    tab, rows_o, white_o, dscr, dbf, filt, left, wv, own,
    sK, rK, sZ, rZ, sY, rY, keepA, keepB, tot, sT, rT, sR, rR,
    table_s, table_r, rows_s, rows_r, white_s, white_r,
    k_s, k_r, z_s, z_r, y_s, y_r, t_s, t_r, r_s, r_r,
):
    c, o = lax.axis_index("coef"), lax.axis_index("obs")
    x, y_hi = c // 2, c % 2
    z, y_lo, k = o // 4, (o // 2) % 2, o % 2
    y = 2 * y_hi + y_lo
    here = 2 * c + y_lo

    def at(xx, yy, zz, kk):
        return {"coef": 2 * xx + yy // 2, "obs": 4 * zz + 2 * (yy % 2) + kk}

    z_odd = z + 1 - 2 * (z % 2)
    sibling = at(x, y, z, 1 - k)
    z_first = at(x, y, z_odd, k)
    z_second = at(x, y, 3 - z, k)
    y_up = at(x, (y + 1) % 4, z, k)
    y_down = at(x, (y + 3) % 4, z, k)
    y_pair = at(x, y + 1 - 2 * y_lo, z, k)
    near = [sibling, z_first, z_second, y_up, y_down]
    near += [{"coef": (c + j) % 8, "obs": o} for j in range(1, 8)]

    def copy(src, dst, send, recv, device):
        return pltpu.make_async_remote_copy(
            src_ref=src, dst_ref=dst, send_sem=send, recv_sem=recv,
            device_id=device, device_id_type=MESH,
        )

    barrier = pltpu.get_barrier_semaphore()
    for device in near:
        pl.semaphore_signal(barrier, inc=1, device_id=device, device_id_type=MESH)
    pl.semaphore_wait(barrier, len(near))

    tables = [
        copy(table_ref, tab.at[pl.ds(2 * c, 2)], table_s.at[j - 1], table_r.at[j - 1],
             {"coef": (c + j) % 8, "obs": o})
        for j in range(1, 8)
    ]
    for t in tables:
        t.start()
    row_copy = copy(rows_ref, rows_o, rows_s, rows_r, y_up)
    row_copy.start()
    parts = [(3, 0), (0, 0), (2, 1), (1, 1)]
    whites = []
    for n, (block, way) in enumerate(parts):
        area = (pl.ds(block * TILE, TILE), pl.ds(0, (block + 1) * TILE))
        whites.append(copy(white_ref.at[area], white_o.at[area], white_s.at[n], white_r.at[n],
                           y_up if way == 0 else y_down))
    for w in whites:
        w.start()
    tab[pl.ds(2 * c, 2)] = table_ref[...]

    parity = (lax.broadcasted_iota(jnp.int32, (8, SEG), 0) % 2).astype(F32)

    def triangular(operand, white, put):
        for block in range(SEG // TILE):
            depth = (block + 1) * TILE
            put(block, lax.dot_general(
                operand[:, :depth], white[pl.ds(block * TILE, TILE), pl.ds(0, depth)], NT,
                preferred_element_type=F32))

    def keep_level(level, value):
        for part in range(8):
            dscr[part, pl.ds(level, 8, stride=PITCH), :] = value[:, part * 128:(part + 1) * 128]

    def make_filtered(rows, white, d, column):
        coefs = tab[(here + d) % NSETS]
        order, log_const = coefs[:, 0:1], coefs[:, 64:65]
        sectorial = math.sqrt(2.0) * jnp.exp(log_const + order * rows[0:1, :])
        cosine = jnp.broadcast_to(rows[1:2, :], (8, SEG))
        turn = order * rows[2:3, :] - 0.25 * parity
        turn = turn - jnp.floor(turn + 0.5)
        square = turn * turn
        harmonic = jnp.full_like(square, COS_TERMS[-1])
        for term in COS_TERMS[-2::-1]:
            harmonic = harmonic * square + term
        lower = sectorial * harmonic
        lowest = jnp.zeros_like(lower)
        keep_level(0, lower)
        for level in range(1, LEV):
            value = (coefs[:, level:level + 1] * cosine) * lower - coefs[:, 64 + level:65 + level] * lowest
            keep_level(level, value)
            lower, lowest = value, lower
        for slot in range(8):
            for part in range(8):
                dbf[slot * LEV:(slot + 1) * LEV, part * 128:(part + 1) * 128] = (
                    dscr[part, slot * PITCH:slot * PITCH + LEV, :].astype(BF16))

        def put(block, value):
            filt[d, :, pl.ds(column + block * TILE, TILE)] = value.astype(BF16)

        triangular(dbf, white, put)

    def make_whitened(rows, white, column):
        pieces = split_rows(rows[3:4, :])

        def put(block, value):
            row = jnp.sum(value, axis=0, keepdims=True)
            wv[:, pl.ds(column + block * TILE, TILE)] = split_rows(row)

        triangular(pieces, white, put)

    make_filtered(rows_ref, white_ref, 0, 0)
    make_whitened(rows_ref, white_ref, 0)
    for t in tables:
        t.wait()

    def first(d, carry):
        make_filtered(rows_ref, white_ref, d, 0)
        return carry

    lax.fori_loop(1, NEAR, first, 0)
    row_copy.wait()
    for w in whites:
        w.wait()
    make_filtered(rows_o, white_o, 0, SEG)
    make_whitened(rows_o, white_o, SEG)
    order_z = [z, 3 - z, 3 - z_odd, z_odd]
    for half, kk in enumerate((1 - k, k)):
        for n, zz in enumerate(order_z):
            left[pl.ds(half * 256 + n * 64, 64), :] = filt[0, pl.ds(pl.multiple_of((2 * zz + kk) * 64, 64), 64), :]

    rhs_part = lax.dot_general(wv[...], filt[0], NT, preferred_element_type=F32)
    rhs_sum = jnp.sum(rhs_part, axis=0, keepdims=True)
    sR[0] = jnp.broadcast_to(rhs_sum, (8, SET))

    def rhs_copy(n):
        return copy(sR.at[n], rR.at[n], r_s.at[n], r_r.at[n], (sibling, z_first, z_second, y_pair)[n])

    rhs_copy(0).start()

    def rhs_step(n):
        rhs_copy(n).wait()
        if n < 3:
            sR[n + 1] = sR[n] + rR[n]
            rhs_copy(n + 1).start()
        else:
            scale = 1.0 / math.sqrt(16.0 * SEG)
            for zz in range(4):
                lanes = slice(zz * 128, (zz + 1) * 128)
                rhs_ref[0:1, pl.ds(pl.multiple_of(zz * 256 + y_lo * 128, 128), 128)] = scale * sR[3, 0:1, lanes]
                rhs_ref[0:1, pl.ds(pl.multiple_of(zz * 256 + (1 - y_lo) * 128, 128), 128)] = scale * rR[3, 0:1, lanes]

    inv_rows = 1.0 / (16.0 * SEG)

    def set_of(j):
        return (j + 1) % NEAR

    def base_of(q):
        return (q // 2) * 1024 + (q % 2) * 128

    def k_copy(j):
        return copy(sK.at[j], rK.at[j], k_s.at[j], k_r.at[j], sibling)

    def z_copies(j):
        return [copy(sZ.at[j, h], rZ.at[j, h], z_s.at[j, h], z_r.at[j, h], (z_first, z_second)[h]) for h in range(2)]

    def y_copies(j):
        return [copy(sY.at[j, h], rY.at[j, h], y_s.at[j, h], y_r.at[j, h], (z_second, z_first)[h]) for h in range(2)]

    def t_copy(j, slot):
        q = (here + j + 1) % NSETS
        return copy(sT.at[j, slot], rT.at[j, 2 * z + k], t_s.at[j, slot], t_r.at[j],
                    at(q // 4, q % 4, slot // 2, slot % 2))

    def finish(j):
        for move in y_copies(j):
            move.wait_recv()
        total = tot[...] + jnp.concatenate([rY[j, 0], rY[j, 1]], axis=1).astype(F32)
        base = base_of((here + set_of(j)) % NSETS)
        for zz in range(4):
            out_ref[:, pl.ds(pl.multiple_of(base + zz * 256, 128), 128)] = inv_rows * total[:, zz * 128:(zz + 1) * 128]

        @pl.when(j < MIRROR)
        def _():
            turned = total.T
            for slot in range(8):
                sT[j, slot] = jnp.concatenate(
                    [turned[slot * 64:slot * 64 + 32], turned[slot * 64 + 32:slot * 64 + 64]], axis=1).astype(BF16)

            def send(slot, carry):
                t_copy(j, slot).start()
                return carry

            lax.fori_loop(0, 8, send, 0)

    def second(j):
        for move in z_copies(j):
            move.wait_recv()
        sY[j, 0] = (keepA[64:128, :] + rZ[j, 0, 0:64, :].astype(F32)).astype(BF16)
        sY[j, 1] = (keepB[64:128, :] + rZ[j, 1, 64:128, :].astype(F32)).astype(BF16)
        for move in y_copies(j):
            move.start()
        tot[:, 0:256] = keepA[0:64, :] + rZ[j, 0, 64:128, :].astype(F32)
        tot[:, 256:512] = keepB[0:64, :] + rZ[j, 1, 0:64, :].astype(F32)

    def third(j):
        k_copy(j).wait_recv()
        sZ[j, 0] = (own[128:256, 0:256] + rK[j, 128:256, 0:256].astype(F32)).astype(BF16)
        sZ[j, 1] = (own[64:192, 256:512] + rK[j, 64:192, 256:512].astype(F32)).astype(BF16)
        for move in z_copies(j):
            move.start()
        keepA[...] = own[0:128, 0:256] + rK[j, 0:128, 0:256].astype(F32)
        keepB[0:64, :] = own[0:64, 256:512] + rK[j, 0:64, 256:512].astype(F32)
        keepB[64:128, :] = own[192:256, 256:512] + rK[j, 192:256, 256:512].astype(F32)

    def gram(j):
        d = set_of(j)
        for n in range(2):
            part = lax.dot_general(left[...], filt[d, n * 256:(n + 1) * 256, :], NT, preferred_element_type=F32)
            sK[j, :, n * 256:(n + 1) * 256] = part[0:256].astype(BF16)
            own[:, n * 256:(n + 1) * 256] = part[256:512]
        k_copy(j).start()

    def stage(i, carry):
        @pl.when(i < NEAR - 1)
        def _():
            make_filtered(rows_o, white_o, i + 1, SEG)

        for n in range(4):
            @pl.when(i == n)
            def _(n=n):
                rhs_step(n)

        @pl.when(i >= 3)
        def _():
            finish(i - 3)

        @pl.when((i >= 2) & (i < NEAR + 2))
        def _():
            second(i - 2)

        @pl.when((i >= 1) & (i < NEAR + 1))
        def _():
            third(i - 1)

        @pl.when(i < NEAR)
        def _():
            gram(i)

        return carry

    lax.fori_loop(0, NEAR + 3, stage, 0)

    def mirrored(j, carry):
        copy(sT.at[j], rT.at[j], t_s.at[j, 0], t_r.at[j], sibling).wait_recv()
        base = base_of((here + NSETS - 1 - j) % NSETS)
        for zz in range(4):
            for half in range(2):
                lanes = slice(half * 64, half * 64 + 64)
                piece = jnp.concatenate(
                    [rT[j, 2 * zz, :, lanes].astype(F32), rT[j, 2 * zz + 1, :, lanes].astype(F32)], axis=1)
                out_ref[half * 32:half * 32 + 32, pl.ds(pl.multiple_of(base + zz * 256, 128), 128)] = inv_rows * piece

        def sent(slot, inner):
            t_copy(j, slot).wait_send()
            return inner

        lax.fori_loop(0, 8, sent, 0)
        return carry

    lax.fori_loop(0, MIRROR, mirrored, 0)

    def drain(j, carry):
        k_copy(j).wait_send()
        for move in z_copies(j) + y_copies(j):
            move.wait_send()
        return carry

    lax.fori_loop(0, NEAR, drain, 0)


def on_device(sample_index, colatitude, longitude, orders, observed, whitening):
    vmem = pl.BlockSpec(memory_space=pltpu.VMEM)
    shaped_orders = orders.reshape(4, 2, 2).transpose(1, 0, 2).reshape(16, 1)
    rows, table = pl.pallas_call(
        prep_kernel,
        out_shape=(jax.ShapeDtypeStruct((8, SEG), F32), jax.ShapeDtypeStruct((16, 128), F32)),
        in_specs=[vmem] * 5,
        out_specs=(vmem, vmem),
    )(
        sample_index.reshape(1, SEG), colatitude.reshape(128, 128), longitude.reshape(128, 128),
        shaped_orders, observed.reshape(1, SEG),
    )
    V = pltpu.VMEM
    dma = pltpu.SemaphoreType.DMA
    normal, rhs = pl.pallas_call(
        main_kernel,
        out_shape=(jax.ShapeDtypeStruct((64, 8192), F32), jax.ShapeDtypeStruct((1, SEG), F32)),
        in_specs=[vmem] * 3,
        out_specs=(vmem, vmem),
        scratch_shapes=[
            V((NSETS, 8, 128), F32), V((8, SEG), F32), V((SEG, SEG), BF16),
            V((8, 8 * PITCH, 128), F32), V((SET, SEG), BF16), V((NEAR, SET, 2 * SEG), BF16),
            V((SET, 2 * SEG), BF16), V((16, 2 * SEG), BF16), V((256, SET), F32),
            V((NEAR, 256, SET), BF16), V((NEAR, 256, SET), BF16),
            V((NEAR, 2, 128, 256), BF16), V((NEAR, 2, 128, 256), BF16),
            V((NEAR, 2, 64, 256), BF16), V((NEAR, 2, 64, 256), BF16),
            V((128, 256), F32), V((128, 256), F32), V((64, SET), F32),
            V((MIRROR, 8, 32, 128), BF16), V((MIRROR, 8, 32, 128), BF16),
            V((4, 8, SET), F32), V((4, 8, SET), F32),
            dma((7,)), dma((7,)), dma, dma, dma((4,)), dma((4,)),
            dma((NEAR,)), dma((NEAR,)), dma((NEAR, 2)), dma((NEAR, 2)),
            dma((NEAR, 2)), dma((NEAR, 2)), dma((MIRROR, 8)), dma((MIRROR,)),
            dma((4,)), dma((4,)),
        ],
        compiler_params=pltpu.CompilerParams(
            collective_id=0, has_side_effects=True, vmem_limit_bytes=58 * 2**20,
        ),
    )(rows, table.reshape(2, 8, 128), whitening)
    return normal, rhs.reshape(SEG)


def solution(mesh):
    placed = (P("obs"), P(), P(), P("coef"), P("obs"), P("obs", None))
    return jax.shard_map(
        on_device,
        mesh=mesh,
        in_specs=placed,
        out_specs=(P(("coef", "obs"), None), P("coef")),
        check_vma=False,
    )
```

time: 819 us -> 89.7 us (0.11)
  the two profiles are of different devices: /device:TPU:1 before, /device:TPU:4 now
where the time goes in v1:
time: 89.7 us; the launch traced here: 89.5 us
  Pallas kernels  83.8 us (93%)
  local copies, waits for them, and re-layouts  5.08 us (6%)
    pallas_call x1, Pallas kernels, on_device(): pl.pallas_call(main_kernel, out_shape=(jax.ShapeDtypeStruct((64, 8192), F...  81.2 us
    unnamed x4, local copies, waits for them, and re-layouts  3.66 us
    pallas_call x1, Pallas kernels, on_device(): pl.pallas_call(prep_kernel, out_shape=(jax.ShapeDtypeStruct((8, SEG), F32...  2.62 us

profile of v1, /device:TPU:4, one launch (start us, length us, event | category | flops | bytes accessed | tf_op | source)
XLA Modules:
  0.0 89.5 jit_solution(17356389248830593655)
XLA Ops:
  0.6 0.7 reshape.31
  1.4 0.7 reshape.36.orders_ref
  2.1 2.6 %shard_map.77 = (f32[8,1024]{1,0:T(8,128)}, f32[16,128]{1,0:T(8,128)}) custom-call(s32[1,1024]{1,0:T(1,128)} %bitcast.11, f32[128,128]{1,0:T(8,128)} %bitcast.7, f32[128,128]{1,0:T(8,128)} %bitcast.8, s32[16,1]{1,0:T(8,128)} %reshape.36.orders_ref, f32[1,1024]{1,0:T(1,128)} %bitcast.12), custom_call_target="tpu_custom_call" | custom-call | tf_op jit(solution)/shard_map/pallas_call | solution.py:357
  4.7 81.2 %shard_map.78 = (f32[64,8192]{1,0:T(8,128)}, f32[1,1024]{1,0:T(1,128)}) custom-call(f32[8,1024]{1,0:T(8,128)} %get-tuple-element.6.rows_ref, f32[2,8,128]{2,1,0:T(8,128)} %bitcast.10, bf16[1024,1024]{1,0:T(8,128)(2,1)} %white_ref.1), custom_call_target="tpu_custom_call" | custom-call | tf_op jit(solution)/shard_map/pallas_call | solution.py:368
  85.8 0.0 copy-start
  85.8 3.1 %copy.14 = f32[64,8192]{1,0:T(8,128)} copy(f32[64,8192]{1,0:T(8,128)} %get-tuple-element.12) | data formatting | bytes 4194304
  88.9 0.0 copy-done
  88.9 0.6 copy.15
  (1 shorter events, 0.0 us)
Async XLA Ops:
  85.8 3.1 %copy-start = (f32[1,1024]{1,0:T(1,128)S(1)}, f32[1,1024]{1,0:T(1,128)}, u32[]{:S(2)}) copy-start(f32[1,1024]{1,0:T(1,128)} %get-tuple-element.9) | copy-start | bytes 12292

commit v2 on v1

--- a/solution.py
+++ b/solution.py
@@ -24,7 +24,7 @@
 COS_TERMS = [(-1.0) ** i * (2.0 * math.pi) ** (2 * i) / math.factorial(2 * i) for i in range(11)]
 
 
-def prep_kernel(index_ref, colat_ref, long_ref, orders_ref, observed_ref, rows_ref, table_ref):
+def prepare(index_ref, colat_ref, long_ref, orders_ref, observed_ref, rows_ref):
     index = index_ref[...]
     high, low = index // 128, index % 128
     pos = lax.broadcasted_iota(jnp.int32, (128, SEG), 0)
@@ -46,7 +46,10 @@
     rows_ref[2:3, :] = longitude * (0.5 / math.pi)
     rows_ref[3:4, :] = observed_ref[...]
 
-    order = orders_ref[...].astype(F32)
+    place = lax.broadcasted_iota(jnp.int32, (16, 16), 0)
+    wanted = (place // 2 % 4) * 4 + (place // 8) * 2 + place % 2
+    given = lax.broadcasted_iota(jnp.int32, (16, 16), 1)
+    order = jnp.sum(jnp.where(given == wanted, orders_ref[...].astype(F32), 0.0), axis=1, keepdims=True)
     counter = (lax.broadcasted_iota(jnp.int32, (16, 384), 1) + 1).astype(F32)
     log_const = jnp.sum(
         jnp.where(counter <= order, 0.5 * jnp.log((2.0 * counter + 1.0) / (2.0 * counter)), 0.0),
@@ -62,7 +65,17 @@
     )
     table = jnp.where(lane < 64, rise, fall)
     table = jnp.where(lane == 0, order, table)
-    table_ref[...] = jnp.where(lane == 64, log_const, table)
+    return jnp.where(lane == 64, log_const, table)
+
+
+def interleave(*parts):
+    parts = list(parts)
+    while parts:
+        for part in list(parts):
+            try:
+                next(part)
+            except StopIteration:
+                parts.remove(part)
 
 
 def split_rows(row):
@@ -76,10 +89,10 @@
 
 
 def main_kernel(
-    rows_ref, table_ref, white_ref, out_ref, rhs_ref,
-    tab, rows_o, white_o, dscr, dbf, filt, left, wv, own,
+    index_ref, colat_ref, long_ref, orders_ref, observed_ref, white_ref, out_ref, rhs_ref,
+    tab, rows_l, rows_o, white_l, white_o, dscr, dbfA, dbfB, filt, left, wv, own,
     sK, rK, sZ, rZ, sY, rY, keepA, keepB, tot, sT, rT, sR, rR,
-    table_s, table_r, rows_s, rows_r, white_s, white_r,
+    load_s, table_s, table_r, rows_s, rows_r, white_s, white_r,
     k_s, k_r, z_s, z_r, y_s, y_r, t_s, t_r, r_s, r_r,
 ):
     c, o = lax.axis_index("coef"), lax.axis_index("obs")
@@ -110,26 +123,28 @@
     barrier = pltpu.get_barrier_semaphore()
     for device in near:
         pl.semaphore_signal(barrier, inc=1, device_id=device, device_id_type=MESH)
+    load = pltpu.make_async_copy(white_ref, white_l, load_s)
+    load.start()
+    table = prepare(index_ref, colat_ref, long_ref, orders_ref, observed_ref, rows_l)
+    tab[2 * c] = table[0:8]
+    tab[2 * c + 1] = table[8:16]
     pl.semaphore_wait(barrier, len(near))
 
-    tables = [
-        copy(table_ref, tab.at[pl.ds(2 * c, 2)], table_s.at[j - 1], table_r.at[j - 1],
-             {"coef": (c + j) % 8, "obs": o})
-        for j in range(1, 8)
-    ]
-    for t in tables:
-        t.start()
-    row_copy = copy(rows_ref, rows_o, rows_s, rows_r, y_up)
+    def table_copy(j):
+        mine = tab.at[pl.ds(2 * c, 2)]
+        return copy(mine, mine, table_s.at[j - 1], table_r.at[j - 1], {"coef": (c + 8 - j) % 8, "obs": o})
+
+    for j in range(1, 5):
+        table_copy(j).start()
+    row_copy = copy(rows_l, rows_o, rows_s, rows_r, y_up)
     row_copy.start()
-    parts = [(3, 0), (0, 0), (2, 1), (1, 1)]
     whites = []
-    for n, (block, way) in enumerate(parts):
+    for n, (block, way) in enumerate([(3, 0), (2, 1), (0, 0), (1, 1)]):
         area = (pl.ds(block * TILE, TILE), pl.ds(0, (block + 1) * TILE))
         whites.append(copy(white_ref.at[area], white_o.at[area], white_s.at[n], white_r.at[n],
                            y_up if way == 0 else y_down))
     for w in whites:
         w.start()
-    tab[pl.ds(2 * c, 2)] = table_ref[...]
 
     parity = (lax.broadcasted_iota(jnp.int32, (8, SEG), 0) % 2).astype(F32)
 
@@ -144,7 +159,7 @@
         for part in range(8):
             dscr[part, pl.ds(level, 8, stride=PITCH), :] = value[:, part * 128:(part + 1) * 128]
 
-    def make_filtered(rows, white, d, column):
+    def design(rows, d, dbf):
         coefs = tab[(here + d) % NSETS]
         order, log_const = coefs[:, 0:1], coefs[:, 64:65]
         sectorial = math.sqrt(2.0) * jnp.exp(log_const + order * rows[0:1, :])
@@ -162,15 +177,21 @@
             value = (coefs[:, level:level + 1] * cosine) * lower - coefs[:, 64 + level:65 + level] * lowest
             keep_level(level, value)
             lower, lowest = value, lower
+            if level % 8 == 7:
+                yield
         for slot in range(8):
             for part in range(8):
                 dbf[slot * LEV:(slot + 1) * LEV, part * 128:(part + 1) * 128] = (
                     dscr[part, slot * PITCH:slot * PITCH + LEV, :].astype(BF16))
-
-        def put(block, value):
+            yield
+
+    def whiten(white, d, dbf, column):
+        for block in range(SEG // TILE):
+            depth = (block + 1) * TILE
+            value = lax.dot_general(
+                dbf[:, :depth], white[block * TILE:(block + 1) * TILE, :depth], NT, preferred_element_type=F32)
             filt[d, :, pl.ds(column + block * TILE, TILE)] = value.astype(BF16)
-
-        triangular(dbf, white, put)
+            yield
 
     def make_whitened(rows, white, column):
         pieces = split_rows(rows[3:4, :])
@@ -181,20 +202,26 @@
 
         triangular(pieces, white, put)
 
-    make_filtered(rows_ref, white_ref, 0, 0)
-    make_whitened(rows_ref, white_ref, 0)
-    for t in tables:
-        t.wait()
-
-    def first(d, carry):
-        make_filtered(rows_ref, white_ref, d, 0)
+    interleave(design(rows_l, 0, dbfA))
+    load.wait()
+    make_whitened(rows_l, white_l, 0)
+
+    def first(t, carry):
+        for j in range(4):
+            @pl.when(t == j)
+            def _(j=j):
+                table_copy(j + 1).wait()
+
+        interleave(whiten(white_l, 2 * t, dbfA, 0), design(rows_l, 2 * t + 1, dbfB))
+        interleave(whiten(white_l, 2 * t + 1, dbfB, 0), design(rows_l, 2 * t + 2, dbfA))
         return carry
 
-    lax.fori_loop(1, NEAR, first, 0)
+    lax.fori_loop(0, 4, first, 0)
     row_copy.wait()
+    interleave(whiten(white_l, 8, dbfA, 0), design(rows_o, 0, dbfB))
     for w in whites:
         w.wait()
-    make_filtered(rows_o, white_o, 0, SEG)
+    interleave(whiten(white_o, 0, dbfB, SEG), design(rows_o, 1, dbfA))
     make_whitened(rows_o, white_o, SEG)
     order_z = [z, 3 - z, 3 - z_odd, z_odd]
     for half, kk in enumerate((1 - k, k)):
@@ -216,13 +243,10 @@
             sR[n + 1] = sR[n] + rR[n]
             rhs_copy(n + 1).start()
         else:
-            scale = 1.0 / math.sqrt(16.0 * SEG)
             for zz in range(4):
                 lanes = slice(zz * 128, (zz + 1) * 128)
-                rhs_ref[0:1, pl.ds(pl.multiple_of(zz * 256 + y_lo * 128, 128), 128)] = scale * sR[3, 0:1, lanes]
-                rhs_ref[0:1, pl.ds(pl.multiple_of(zz * 256 + (1 - y_lo) * 128, 128), 128)] = scale * rR[3, 0:1, lanes]
-
-    inv_rows = 1.0 / (16.0 * SEG)
+                rhs_ref[0:1, pl.ds(pl.multiple_of(zz * 256 + y_lo * 128, 128), 128)] = sR[3, 0:1, lanes]
+                rhs_ref[0:1, pl.ds(pl.multiple_of(zz * 256 + (1 - y_lo) * 128, 128), 128)] = rR[3, 0:1, lanes]
 
     def set_of(j):
         return (j + 1) % NEAR
@@ -247,13 +271,12 @@
     def finish(j):
         for move in y_copies(j):
             move.wait_recv()
-        total = tot[...] + jnp.concatenate([rY[j, 0], rY[j, 1]], axis=1).astype(F32)
+        total = tot[j % 2] + jnp.concatenate([rY[j, 0], rY[j, 1]], axis=1).astype(F32)
         base = base_of((here + set_of(j)) % NSETS)
         for zz in range(4):
-            out_ref[:, pl.ds(pl.multiple_of(base + zz * 256, 128), 128)] = inv_rows * total[:, zz * 128:(zz + 1) * 128]
-
-        @pl.when(j < MIRROR)
-        def _():
+            out_ref[:, pl.ds(pl.multiple_of(base + zz * 256, 128), 128)] = total[:, zz * 128:(zz + 1) * 128]
+
+        def mirror():
             turned = total.T
             for slot in range(8):
                 sT[j, slot] = jnp.concatenate(
@@ -265,63 +288,74 @@
 
             lax.fori_loop(0, 8, send, 0)
 
+        if not isinstance(j, int) or j < MIRROR:
+            mirror()
+
     def second(j):
+        par = j % 2
         for move in z_copies(j):
             move.wait_recv()
-        sY[j, 0] = (keepA[64:128, :] + rZ[j, 0, 0:64, :].astype(F32)).astype(BF16)
-        sY[j, 1] = (keepB[64:128, :] + rZ[j, 1, 64:128, :].astype(F32)).astype(BF16)
+        sY[j, 0] = (keepA[par, 64:128, :] + rZ[j, 0, 0:64, :].astype(F32)).astype(BF16)
+        sY[j, 1] = (keepB[par, 64:128, :] + rZ[j, 1, 64:128, :].astype(F32)).astype(BF16)
         for move in y_copies(j):
             move.start()
-        tot[:, 0:256] = keepA[0:64, :] + rZ[j, 0, 64:128, :].astype(F32)
-        tot[:, 256:512] = keepB[0:64, :] + rZ[j, 1, 0:64, :].astype(F32)
+        tot[par, :, 0:256] = keepA[par, 0:64, :] + rZ[j, 0, 64:128, :].astype(F32)
+        tot[par, :, 256:512] = keepB[par, 0:64, :] + rZ[j, 1, 0:64, :].astype(F32)
 
     def third(j):
+        par = j % 2
         k_copy(j).wait_recv()
-        sZ[j, 0] = (own[128:256, 0:256] + rK[j, 128:256, 0:256].astype(F32)).astype(BF16)
-        sZ[j, 1] = (own[64:192, 256:512] + rK[j, 64:192, 256:512].astype(F32)).astype(BF16)
+        sZ[j, 0] = (own[par, 128:256, 0:256] + rK[j, 128:256, 0:256].astype(F32)).astype(BF16)
+        sZ[j, 1] = (own[par, 64:192, 256:512] + rK[j, 64:192, 256:512].astype(F32)).astype(BF16)
         for move in z_copies(j):
             move.start()
-        keepA[...] = own[0:128, 0:256] + rK[j, 0:128, 0:256].astype(F32)
-        keepB[0:64, :] = own[0:64, 256:512] + rK[j, 0:64, 256:512].astype(F32)
-        keepB[64:128, :] = own[192:256, 256:512] + rK[j, 192:256, 256:512].astype(F32)
-
-    def gram(j):
-        d = set_of(j)
+        keepA[par] = own[par, 0:128, 0:256] + rK[j, 0:128, 0:256].astype(F32)
+        keepB[par, 0:64, :] = own[par, 0:64, 256:512] + rK[j, 0:64, 256:512].astype(F32)
+        keepB[par, 64:128, :] = own[par, 192:256, 256:512] + rK[j, 192:256, 256:512].astype(F32)
+
+    def gram(j, d):
         for n in range(2):
             part = lax.dot_general(left[...], filt[d, n * 256:(n + 1) * 256, :], NT, preferred_element_type=F32)
             sK[j, :, n * 256:(n + 1) * 256] = part[0:256].astype(BF16)
-            own[:, n * 256:(n + 1) * 256] = part[256:512]
-        k_copy(j).start()
+            own[j % 2, :, n * 256:(n + 1) * 256] = part[256:512]
+            yield
 
     def stage(i, carry):
-        @pl.when(i < NEAR - 1)
-        def _():
-            make_filtered(rows_o, white_o, i + 1, SEG)
-
         for n in range(4):
             @pl.when(i == n)
             def _(n=n):
                 rhs_step(n)
 
+        @pl.when(i >= 2)
+        def _():
+            third(i - 2)
+
+        interleave(whiten(white_o, i + 1, dbfA, SEG))
+
         @pl.when(i >= 3)
         def _():
-            finish(i - 3)
-
-        @pl.when((i >= 2) & (i < NEAR + 2))
+            second(i - 3)
+
+        @pl.when(i >= 4)
         def _():
-            second(i - 2)
-
-        @pl.when((i >= 1) & (i < NEAR + 1))
-        def _():
-            third(i - 1)
-
-        @pl.when(i < NEAR)
-        def _():
-            gram(i)
-
+            finish(i - 4)
+
+        interleave(gram(i, i + 1), design(rows_o, jnp.minimum(i + 2, NEAR - 1), dbfA))
+        k_copy(i).start()
         return carry
 
-    lax.fori_loop(0, NEAR + 3, stage, 0)
+    lax.fori_loop(0, NEAR - 1, stage, 0)
+    third(6)
+    interleave(gram(8, 0))
+    k_copy(8).start()
+    second(5)
+    finish(4)
+    third(7)
+    second(6)
+    finish(5)
+    third(8)
+    second(7)
+    finish(6)
 
     def mirrored(j, carry):
         copy(sT.at[j], rT.at[j], t_s.at[j, 0], t_r.at[j], sibling).wait_recv()
@@ -331,7 +365,7 @@
                 lanes = slice(half * 64, half * 64 + 64)
                 piece = jnp.concatenate(
                     [rT[j, 2 * zz, :, lanes].astype(F32), rT[j, 2 * zz + 1, :, lanes].astype(F32)], axis=1)
-                out_ref[half * 32:half * 32 + 32, pl.ds(pl.multiple_of(base + zz * 256, 128), 128)] = inv_rows * piece
+                out_ref[half * 32:half * 32 + 32, pl.ds(pl.multiple_of(base + zz * 256, 128), 128)] = piece
 
         def sent(slot, inner):
             t_copy(j, slot).wait_send()
@@ -340,7 +374,12 @@
         lax.fori_loop(0, 8, sent, 0)
         return carry
 
-    lax.fori_loop(0, MIRROR, mirrored, 0)
+    lax.fori_loop(0, 3, mirrored, 0)
+    second(8)
+    finish(7)
+    lax.fori_loop(3, 5, mirrored, 0)
+    finish(8)
+    lax.fori_loop(5, MIRROR, mirrored, 0)
 
     def drain(j, carry):
         k_copy(j).wait_send()
@@ -353,43 +392,39 @@
 
 def on_device(sample_index, colatitude, longitude, orders, observed, whitening):
     vmem = pl.BlockSpec(memory_space=pltpu.VMEM)
-    shaped_orders = orders.reshape(4, 2, 2).transpose(1, 0, 2).reshape(16, 1)
-    rows, table = pl.pallas_call(
-        prep_kernel,
-        out_shape=(jax.ShapeDtypeStruct((8, SEG), F32), jax.ShapeDtypeStruct((16, 128), F32)),
-        in_specs=[vmem] * 5,
-        out_specs=(vmem, vmem),
-    )(
-        sample_index.reshape(1, SEG), colatitude.reshape(128, 128), longitude.reshape(128, 128),
-        shaped_orders, observed.reshape(1, SEG),
-    )
     V = pltpu.VMEM
     dma = pltpu.SemaphoreType.DMA
     normal, rhs = pl.pallas_call(
         main_kernel,
         out_shape=(jax.ShapeDtypeStruct((64, 8192), F32), jax.ShapeDtypeStruct((1, SEG), F32)),
-        in_specs=[vmem] * 3,
+        in_specs=[vmem] * 5 + [pl.BlockSpec(memory_space=pl.ANY)],
         out_specs=(vmem, vmem),
         scratch_shapes=[
-            V((NSETS, 8, 128), F32), V((8, SEG), F32), V((SEG, SEG), BF16),
-            V((8, 8 * PITCH, 128), F32), V((SET, SEG), BF16), V((NEAR, SET, 2 * SEG), BF16),
-            V((SET, 2 * SEG), BF16), V((16, 2 * SEG), BF16), V((256, SET), F32),
+            V((NSETS, 8, 128), F32), V((8, SEG), F32), V((8, SEG), F32),
+            V((SEG, SEG), BF16), V((SEG, SEG), BF16),
+            V((8, 8 * PITCH, 128), F32), V((SET, SEG), BF16), V((SET, SEG), BF16),
+            V((NEAR, SET, 2 * SEG), BF16),
+            V((SET, 2 * SEG), BF16), V((16, 2 * SEG), BF16), V((2, 256, SET), F32),
             V((NEAR, 256, SET), BF16), V((NEAR, 256, SET), BF16),
             V((NEAR, 2, 128, 256), BF16), V((NEAR, 2, 128, 256), BF16),
             V((NEAR, 2, 64, 256), BF16), V((NEAR, 2, 64, 256), BF16),
-            V((128, 256), F32), V((128, 256), F32), V((64, SET), F32),
+            V((2, 128, 256), F32), V((2, 128, 256), F32), V((2, 64, SET), F32),
             V((MIRROR, 8, 32, 128), BF16), V((MIRROR, 8, 32, 128), BF16),
             V((4, 8, SET), F32), V((4, 8, SET), F32),
-            dma((7,)), dma((7,)), dma, dma, dma((4,)), dma((4,)),
+            dma, dma((4,)), dma((4,)), dma, dma, dma((4,)), dma((4,)),
             dma((NEAR,)), dma((NEAR,)), dma((NEAR, 2)), dma((NEAR, 2)),
             dma((NEAR, 2)), dma((NEAR, 2)), dma((MIRROR, 8)), dma((MIRROR,)),
             dma((4,)), dma((4,)),
         ],
         compiler_params=pltpu.CompilerParams(
-            collective_id=0, has_side_effects=True, vmem_limit_bytes=58 * 2**20,
+            collective_id=0, has_side_effects=True, vmem_limit_bytes=60 * 2**20,
         ),
-    )(rows, table.reshape(2, 8, 128), whitening)
-    return normal, rhs.reshape(SEG)
+    )(
+        sample_index.reshape(1, SEG), colatitude.reshape(128, 128), longitude.reshape(128, 128),
+        orders.reshape(1, 16), observed.reshape(1, SEG), whitening,
+    )
+    rows = 16.0 * SEG
+    return normal * (1.0 / rows), rhs.reshape(SEG) * (1.0 / math.sqrt(rows))
 
 
 def solution(mesh):

time: 89.7 us -> 75.6 us (0.84)
  the two profiles are of different devices: /device:TPU:4 before, /device:TPU:1 now
where the time goes in v2:
time: 75.6 us; the launch traced here: 75.4 us
  Pallas kernels  71.1 us (94%)
  other arithmetic  3.66 us (5%)
    pallas_call x1, Pallas kernels, on_device(): pl.pallas_call(main_kernel, out_shape=(jax.ShapeDtypeStruct((64, 8192), F...  71.1 us
    mul x2, other arithmetic, on_device(): return (normal * (1.0 / rows), rhs.reshape(SEG) * (1.0 / math.sqrt(rows)))  3.66 us

profile of v2, /device:TPU:1, one launch (start us, length us, event | category | flops | bytes accessed | tf_op | source)
XLA Modules:
  0.0 75.4 jit_solution(889477963853280633)
XLA Ops:
  0.6 71.1 %shard_map.77 = (f32[64,8192]{1,0:T(8,128)}, f32[1,1024]{1,0:T(1,128)}) custom-call(s32[1,1024]{1,0:T(1,128)} %bitcast.8, f32[128,128]{1,0:T(8,128)} %bitcast.6, f32[128,128]{1,0:T(8,128)} %bitcast.7, s32[1,16]{1,0:T(1,128)} %bitcast.11, f32[1,1024]{1,0:T(1,128)} %bitcast.9, bf16[1024,1024]{1,0:T(8,128)(2,1)} %white_ref.1), custom_call_target="tpu_custom_call" | custom-call | tf_op jit(solution)/shard_map/pallas_call | solution.py:397
  71.7 0.0 copy-start
  71.8 3.1 %broadcast_multiply_fusion = f32[64,8192]{1,0:T(8,128)} fusion(f32[64,8192]{1,0:T(8,128)} %get-tuple-element.4), kind=kLoop, calls=%fused_computation | loop fusion | flops 524288 | bytes 4194304 | tf_op jit(solution)/shard_map/mul | solution.py:427
  74.8 0.0 copy-done
  74.8 0.6 broadcast_multiply_fusion.1
Async XLA Ops:
  71.7 3.1 %copy-start = (f32[1,1024]{1,0:T(1,128)S(1)}, f32[1,1024]{1,0:T(1,128)}, u32[]{:S(2)}) copy-start(f32[1,1024]{1,0:T(1,128)} %get-tuple-element.5) | copy-start | bytes 12292

commit v3 on v2

--- a/solution.py
+++ b/solution.py
@@ -90,7 +90,7 @@
 
 def main_kernel(
     index_ref, colat_ref, long_ref, orders_ref, observed_ref, white_ref, out_ref, rhs_ref,
-    tab, rows_l, rows_o, white_l, white_o, dscr, dbfA, dbfB, filt, left, wv, own,
+    tab, rows_l, rows_o, white_l, white_o, dscr, dbf, filt, part, left, wv, own,
     sK, rK, sZ, rZ, sY, rY, keepA, keepB, tot, sT, rT, sR, rR,
     load_s, table_s, table_r, rows_s, rows_r, white_s, white_r,
     k_s, k_r, z_s, z_r, y_s, y_r, t_s, t_r, r_s, r_r,
@@ -159,7 +159,7 @@
         for part in range(8):
             dscr[part, pl.ds(level, 8, stride=PITCH), :] = value[:, part * 128:(part + 1) * 128]
 
-    def design(rows, d, dbf):
+    def design(rows, d):
         coefs = tab[(here + d) % NSETS]
         order, log_const = coefs[:, 0:1], coefs[:, 64:65]
         sectorial = math.sqrt(2.0) * jnp.exp(log_const + order * rows[0:1, :])
@@ -185,57 +185,72 @@
                     dscr[part, slot * PITCH:slot * PITCH + LEV, :].astype(BF16))
             yield
 
-    def whiten(white, d, dbf, column):
+    def whiten(white):
         for block in range(SEG // TILE):
             depth = (block + 1) * TILE
             value = lax.dot_general(
                 dbf[:, :depth], white[block * TILE:(block + 1) * TILE, :depth], NT, preferred_element_type=F32)
-            filt[d, :, pl.ds(column + block * TILE, TILE)] = value.astype(BF16)
-            yield
-
-    def make_whitened(rows, white, column):
+            filt[:, block * TILE:(block + 1) * TILE] = value.astype(BF16)
+
+    def make_whitened(rows, white):
         pieces = split_rows(rows[3:4, :])
 
         def put(block, value):
             row = jnp.sum(value, axis=0, keepdims=True)
-            wv[:, pl.ds(column + block * TILE, TILE)] = split_rows(row)
+            wv[:, block * TILE:(block + 1) * TILE] = split_rows(row)
 
         triangular(pieces, white, put)
 
-    interleave(design(rows_l, 0, dbfA))
+    def rhs_terms():
+        terms = lax.dot_general(wv[...], filt[...], NT, preferred_element_type=F32)
+        return jnp.broadcast_to(jnp.sum(terms, axis=0, keepdims=True), (8, SET))
+
+    order_z = [z, 3 - z, 3 - z_odd, z_odd]
+
+    def keep_left(column):
+        for half, kk in enumerate((1 - k, k)):
+            for n, zz in enumerate(order_z):
+                left[half * 256 + n * 64:half * 256 + n * 64 + 64, column:column + SEG] = (
+                    filt[pl.ds(pl.multiple_of((2 * zz + kk) * 64, 64), 64), :])
+
+    def product(n, column):
+        return lax.dot_general(left[:, column:column + SEG], filt[n * 256:(n + 1) * 256, :], NT, preferred_element_type=F32)
+
+    def own_terms(d):
+        for n in range(2):
+            part[d, :, n * 256:(n + 1) * 256] = product(n, 0)
+            yield
+
+    interleave(design(rows_l, 0))
     load.wait()
-    make_whitened(rows_l, white_l, 0)
-
-    def first(t, carry):
+    make_whitened(rows_l, white_l)
+
+    def own_stage(d, carry):
+        whiten(white_l)
+
+        @pl.when(d == 0)
+        def _():
+            keep_left(0)
+            sR[0] = rhs_terms()
+
         for j in range(4):
-            @pl.when(t == j)
+            @pl.when(d == 2 * j)
             def _(j=j):
                 table_copy(j + 1).wait()
 
-        interleave(whiten(white_l, 2 * t, dbfA, 0), design(rows_l, 2 * t + 1, dbfB))
-        interleave(whiten(white_l, 2 * t + 1, dbfB, 0), design(rows_l, 2 * t + 2, dbfA))
+        interleave(own_terms(d), design(rows_l, d + 1))
         return carry
 
-    lax.fori_loop(0, 4, first, 0)
+    lax.fori_loop(0, NEAR - 1, own_stage, 0)
+    whiten(white_l)
     row_copy.wait()
-    interleave(whiten(white_l, 8, dbfA, 0), design(rows_o, 0, dbfB))
+    interleave(own_terms(NEAR - 1), design(rows_o, 0))
     for w in whites:
         w.wait()
-    interleave(whiten(white_o, 0, dbfB, SEG), design(rows_o, 1, dbfA))
-    make_whitened(rows_o, white_o, SEG)
-    order_z = [z, 3 - z, 3 - z_odd, z_odd]
-    for half, kk in enumerate((1 - k, k)):
-        for n, zz in enumerate(order_z):
-            left[pl.ds(half * 256 + n * 64, 64), :] = filt[0, pl.ds(pl.multiple_of((2 * zz + kk) * 64, 64), 64), :]
-
-    rhs_part = lax.dot_general(wv[...], filt[0], NT, preferred_element_type=F32)
-    rhs_sum = jnp.sum(rhs_part, axis=0, keepdims=True)
-    sR[0] = jnp.broadcast_to(rhs_sum, (8, SET))
+    make_whitened(rows_o, white_o)
 
     def rhs_copy(n):
         return copy(sR.at[n], rR.at[n], r_s.at[n], r_r.at[n], (sibling, z_first, z_second, y_pair)[n])
-
-    rhs_copy(0).start()
 
     def rhs_step(n):
         rhs_copy(n).wait()
@@ -248,8 +263,7 @@
                 rhs_ref[0:1, pl.ds(pl.multiple_of(zz * 256 + y_lo * 128, 128), 128)] = sR[3, 0:1, lanes]
                 rhs_ref[0:1, pl.ds(pl.multiple_of(zz * 256 + (1 - y_lo) * 128, 128), 128)] = rR[3, 0:1, lanes]
 
-    def set_of(j):
-        return (j + 1) % NEAR
+    inv_rows = 1.0 / (16.0 * SEG)
 
     def base_of(q):
         return (q // 2) * 1024 + (q % 2) * 128
@@ -271,25 +285,28 @@
     def finish(j):
         for move in y_copies(j):
             move.wait_recv()
-        total = tot[j % 2] + jnp.concatenate([rY[j, 0], rY[j, 1]], axis=1).astype(F32)
-        base = base_of((here + set_of(j)) % NSETS)
+        total = inv_rows * (tot[j % 2] + jnp.concatenate([rY[j, 0], rY[j, 1]], axis=1).astype(F32))
+        base = base_of((here + j) % NSETS)
         for zz in range(4):
             out_ref[:, pl.ds(pl.multiple_of(base + zz * 256, 128), 128)] = total[:, zz * 128:(zz + 1) * 128]
 
         def mirror():
             turned = total.T
             for slot in range(8):
-                sT[j, slot] = jnp.concatenate(
+                sT[j - 1, slot] = jnp.concatenate(
                     [turned[slot * 64:slot * 64 + 32], turned[slot * 64 + 32:slot * 64 + 64]], axis=1).astype(BF16)
 
             def send(slot, carry):
-                t_copy(j, slot).start()
+                t_copy(j - 1, slot).start()
                 return carry
 
             lax.fori_loop(0, 8, send, 0)
 
-        if not isinstance(j, int) or j < MIRROR:
-            mirror()
+        if isinstance(j, int):
+            if 1 <= j <= MIRROR:
+                mirror()
+        else:
+            pl.when(j >= 1)(mirror)
 
     def second(j):
         par = j % 2
@@ -313,49 +330,13 @@
         keepB[par, 0:64, :] = own[par, 0:64, 256:512] + rK[j, 0:64, 256:512].astype(F32)
         keepB[par, 64:128, :] = own[par, 192:256, 256:512] + rK[j, 192:256, 256:512].astype(F32)
 
-    def gram(j, d):
+    def gram(j):
         for n in range(2):
-            part = lax.dot_general(left[...], filt[d, n * 256:(n + 1) * 256, :], NT, preferred_element_type=F32)
-            sK[j, :, n * 256:(n + 1) * 256] = part[0:256].astype(BF16)
-            own[j % 2, :, n * 256:(n + 1) * 256] = part[256:512]
+            lanes = slice(n * 256, (n + 1) * 256)
+            total = part[j, :, lanes] + product(n, SEG)
+            sK[j, :, lanes] = total[0:256].astype(BF16)
+            own[j % 2, :, lanes] = total[256:512]
             yield
-
-    def stage(i, carry):
-        for n in range(4):
-            @pl.when(i == n)
-            def _(n=n):
-                rhs_step(n)
-
-        @pl.when(i >= 2)
-        def _():
-            third(i - 2)
-
-        interleave(whiten(white_o, i + 1, dbfA, SEG))
-
-        @pl.when(i >= 3)
-        def _():
-            second(i - 3)
-
-        @pl.when(i >= 4)
-        def _():
-            finish(i - 4)
-
-        interleave(gram(i, i + 1), design(rows_o, jnp.minimum(i + 2, NEAR - 1), dbfA))
-        k_copy(i).start()
-        return carry
-
-    lax.fori_loop(0, NEAR - 1, stage, 0)
-    third(6)
-    interleave(gram(8, 0))
-    k_copy(8).start()
-    second(5)
-    finish(4)
-    third(7)
-    second(6)
-    finish(5)
-    third(8)
-    second(7)
-    finish(6)
 
     def mirrored(j, carry):
         copy(sT.at[j], rT.at[j], t_s.at[j, 0], t_r.at[j], sibling).wait_recv()
@@ -374,6 +355,40 @@
         lax.fori_loop(0, 8, sent, 0)
         return carry
 
+    def stage(i, carry):
+        whiten(white_o)
+
+        @pl.when(i == 0)
+        def _():
+            keep_left(SEG)
+            sR[0] = sR[0] + rhs_terms()
+            rhs_copy(0).start()
+
+        for n in range(4):
+            @pl.when(i == n + 1)
+            def _(n=n):
+                rhs_step(n)
+
+        @pl.when(i >= 1)
+        def _():
+            third(i - 1)
+
+        @pl.when(i >= 2)
+        def _():
+            second(i - 2)
+
+        @pl.when(i >= 3)
+        def _():
+            finish(i - 3)
+
+        interleave(gram(i), design(rows_o, jnp.minimum(i + 1, NEAR - 1)))
+        k_copy(i).start()
+        return carry
+
+    lax.fori_loop(0, NEAR, stage, 0)
+    third(8)
+    second(7)
+    finish(6)
     lax.fori_loop(0, 3, mirrored, 0)
     second(8)
     finish(7)
@@ -381,6 +396,7 @@
     finish(8)
     lax.fori_loop(5, MIRROR, mirrored, 0)
 
+
     def drain(j, carry):
         k_copy(j).wait_send()
         for move in z_copies(j) + y_copies(j):
@@ -388,6 +404,18 @@
         return carry
 
     lax.fori_loop(0, NEAR, drain, 0)
+
+
+def hand_over(normal_ref, rhs_ref, normal_out, rhs_out, sems):
+    moves = [
+        pltpu.make_async_copy(normal_ref.at[pl.ds(n * 16, 16)], normal_out.at[pl.ds(n * 16, 16)], sems.at[n])
+        for n in range(4)
+    ]
+    for move in moves:
+        move.start()
+    rhs_out[...] = rhs_ref[...] * (1.0 / math.sqrt(16.0 * SEG))
+    for move in moves:
+        move.wait()
 
 
 def on_device(sample_index, colatitude, longitude, orders, observed, whitening):
@@ -403,8 +431,8 @@
             V((NSETS, 8, 128), F32), V((8, SEG), F32), V((8, SEG), F32),
             V((SEG, SEG), BF16), V((SEG, SEG), BF16),
             V((8, 8 * PITCH, 128), F32), V((SET, SEG), BF16), V((SET, SEG), BF16),
-            V((NEAR, SET, 2 * SEG), BF16),
-            V((SET, 2 * SEG), BF16), V((16, 2 * SEG), BF16), V((2, 256, SET), F32),
+            V((NEAR, SET, SET), F32),
+            V((SET, 2 * SEG), BF16), V((16, SEG), BF16), V((2, 256, SET), F32),
             V((NEAR, 256, SET), BF16), V((NEAR, 256, SET), BF16),
             V((NEAR, 2, 128, 256), BF16), V((NEAR, 2, 128, 256), BF16),
             V((NEAR, 2, 64, 256), BF16), V((NEAR, 2, 64, 256), BF16),
@@ -423,8 +451,15 @@
         sample_index.reshape(1, SEG), colatitude.reshape(128, 128), longitude.reshape(128, 128),
         orders.reshape(1, 16), observed.reshape(1, SEG), whitening,
     )
-    rows = 16.0 * SEG
-    return normal * (1.0 / rows), rhs.reshape(SEG) * (1.0 / math.sqrt(rows))
+    hbm = pl.BlockSpec(memory_space=pl.ANY)
+    normal, rhs = pl.pallas_call(
+        hand_over,
+        out_shape=(jax.ShapeDtypeStruct((64, 8192), F32), jax.ShapeDtypeStruct((1, SEG), F32)),
+        in_specs=[hbm, vmem],
+        out_specs=(hbm, vmem),
+        scratch_shapes=[dma((4,))],
+    )(normal, rhs)
+    return normal, rhs.reshape(SEG)
 
 
 def solution(mesh):

time: 75.6 us -> 144 us (1.90)
  Pallas kernels: 71.1 us -> 142 us
  other arithmetic: 3.66 us -> 0 us
    pallas_call x0 -> x1, Pallas kernels: none -> 65.9 us  [on_device(): pl.pallas_call(hand_over, out_shape=(jax.ShapeDtypeStruct((64, 8192), F32...]
    pallas_call x1, Pallas kernels: 71.1 us -> 76.1 us  [on_device(): pl.pallas_call(main_kernel, out_shape=(jax.ShapeDtypeStruct((64, 8192), F...]
    mul x2 -> x0, other arithmetic: 3.66 us -> none  [on_device(): return (normal * (1.0 / rows), rhs.reshape(SEG) * (1.0 / math.sqrt(rows)))]
where the time goes in v3:
time: 144 us; the launch traced here: 143 us
  Pallas kernels  142 us (99%)
    pallas_call x1, Pallas kernels, on_device(): pl.pallas_call(main_kernel, out_shape=(jax.ShapeDtypeStruct((64, 8192), F...  76.1 us
    pallas_call x1, Pallas kernels, on_device(): pl.pallas_call(hand_over, out_shape=(jax.ShapeDtypeStruct((64, 8192), F32...  65.9 us

profile of v3, /device:TPU:1, one launch (start us, length us, event | category | flops | bytes accessed | tf_op | source)
XLA Modules:
  0.0 142.7 jit_solution(469936959032624543)
XLA Ops:
  0.6 76.1 %shard_map.77 = (f32[64,8192]{1,0:T(8,128)}, f32[1,1024]{1,0:T(1,128)}) custom-call(s32[1,1024]{1,0:T(1,128)} %bitcast.8, f32[128,128]{1,0:T(8,128)} %bitcast.6, f32[128,128]{1,0:T(8,128)} %bitcast.7, s32[1,16]{1,0:T(1,128)} %bitcast.10, f32[1,1024]{1,0:T(1,128)} %bitcast.9, bf16[1024,1024]{1,0:T(8,128)(2,1)} %white_ref.1), custom_call_target="tpu_custom_call" | custom-call | tf_op jit(solution)/shard_map/pallas_call | solution.py:425
  76.7 65.9 %shard_map.78 = (f32[64,8192]{1,0:T(8,128)}, f32[1,1024]{1,0:T(1,128)}) custom-call(f32[64,8192]{1,0:T(8,128)} %get-tuple-element.6.normal_ref, f32[1,1024]{1,0:T(1,128)} %get-tuple-element.7.rhs_ref), custom_call_target="tpu_custom_call" | custom-call | tf_op jit(solution)/shard_map/pallas_call | solution.py:455

commit v4 on v3

v4 whole, which is shorter than its diff:
```python
import functools
import math

import jax
import jax.numpy as jnp
from jax import lax
from jax.experimental import pallas as pl
from jax.experimental.pallas import tpu as pltpu
from jax.sharding import PartitionSpec as P

LEV = 64
NMAX = 300
SEG = 1024
SET = 512
NSETS = 16
NEAR = 9
MIRROR = 7
TILE = 256
PITCH = 65
F32 = jnp.float32
BF16 = jnp.bfloat16
MESH = pl.DeviceIdType.MESH
NT = (((1,), (1,)), ((), ()))
COS_TERMS = [(-1.0) ** i * (2.0 * math.pi) ** (2 * i) / math.factorial(2 * i) for i in range(11)]


def prepare(index_ref, colat_ref, long_ref, observed_ref, rows_ref):
    index = index_ref[...]
    high, low = index // 128, index % 128
    pos = lax.broadcasted_iota(jnp.int32, (128, SEG), 0)
    pick_high = (pos == high).astype(F32)
    pick_low = (pos == low).astype(F32)

    def look_up(table):
        found = lax.dot_general(
            table, pick_high, (((0,), (0,)), ((), ())),
            precision=lax.Precision.HIGHEST, preferred_element_type=F32,
        )
        return jnp.sum(found * pick_low, axis=0, keepdims=True)

    colat = look_up(colat_ref[...])
    longitude = look_up(long_ref[...])
    rows_ref[...] = jnp.zeros(rows_ref.shape, F32)
    rows_ref[0:1, :] = jnp.log(jnp.sin(colat))
    rows_ref[1:2, :] = jnp.cos(colat)
    rows_ref[2:3, :] = longitude * (0.5 / math.pi)
    rows_ref[3:4, :] = observed_ref[...]


def make_table(orders_ref):
    place = lax.broadcasted_iota(jnp.int32, (16, 16), 0)
    wanted = (place // 2 % 4) * 4 + (place // 8) * 2 + place % 2
    given = lax.broadcasted_iota(jnp.int32, (16, 16), 1)
    order = jnp.sum(jnp.where(given == wanted, orders_ref[...].astype(F32), 0.0), axis=1, keepdims=True)
    counter = (lax.broadcasted_iota(jnp.int32, (16, 384), 1) + 1).astype(F32)
    log_const = jnp.sum(
        jnp.where(counter <= order, 0.5 * jnp.log((2.0 * counter + 1.0) / (2.0 * counter)), 0.0),
        axis=1, keepdims=True,
    )
    lane = lax.broadcasted_iota(jnp.int32, (16, 128), 1)
    step = jnp.maximum(lane % 64, 1).astype(F32)
    degree = order + step
    rise = jnp.sqrt((2.0 * degree - 1.0) * (2.0 * degree + 1.0) / (step * (degree + order)))
    fall = jnp.sqrt(
        (2.0 * degree + 1.0) * (degree + order - 1.0) * (step - 1.0)
        / ((2.0 * degree - 3.0) * (degree + order) * step)
    )
    table = jnp.where(lane < 64, rise, fall)
    table = jnp.where(lane == 0, order, table)
    return jnp.where(lane == 64, log_const, table)


def in_turn(*parts):
    for part in parts:
        yield from part


def chip_of(q):
    high, low = q // 4, q % 4
    return (high + 2 * low) % 4, (high + 3 * low) % 4


def set_of(j):
    return 8 - (j + 1) % 8


def interleave(*parts):
    parts = list(parts)
    while parts:
        for part in list(parts):
            try:
                next(part)
            except StopIteration:
                parts.remove(part)


def split_rows(row):
    high = row.astype(BF16).astype(F32)
    rest = row - high
    middle = rest.astype(BF16).astype(F32)
    low = rest - middle
    place = lax.broadcasted_iota(jnp.int32, (16, row.shape[1]), 0)
    pieces = jnp.where(place == 0, high, jnp.where(place == 1, middle, jnp.where(place == 2, low, 0.0)))
    return pieces.astype(BF16)


def main_kernel(
    index_ref, colat_ref, long_ref, orders_ref, observed_ref, white_ref, out_ref, rhs_ref,
    tab, rows_l, rows_o, white_l, white_o, dscr, dbf, dbf0, filt, filt0, part, left, wv, own,
    sK, rK, sZ, rZ, sY, rY, keepA, keepB, keepD, tot, sD, rD, sT, rT, sR, rR,
    load_s, table_s, table_r, rows_s, rows_r, white_s, white_r,
    k_s, k_r, z_s, z_r, y_s, y_r, d_s, d_r, t_s, t_r, r_s, r_r,
):
    c, o = lax.axis_index("coef"), lax.axis_index("obs")
    x, y_hi = c // 2, c % 2
    z, y_lo, k = o // 4, (o // 2) % 2, o % 2
    y = 2 * y_hi + y_lo
    low = (y - x + 4) % 4
    here = 4 * ((x + 8 - 2 * low) % 4) + low

    def at(xx, yy, zz, kk):
        return {"coef": 2 * xx + yy // 2, "obs": 4 * zz + 2 * (yy % 2) + kk}

    z_odd = z + 1 - 2 * (z % 2)
    sibling = at(x, y, z, 1 - k)
    z_first = at(x, y, z_odd, k)
    z_second = at(x, y, 3 - z, k)
    y_up = at(x, (y + 1) % 4, z, k)
    y_down = at(x, (y + 3) % 4, z, k)
    y_pair = at(x, y + 1 - 2 * y_lo, z, k)
    z_far = at(x, y, (z + 2) % 4, k)
    near = [sibling, z_first, z_second, z_far, y_up, y_down]
    near += [{"coef": (c + j) % 8, "obs": o} for j in range(1, 8)]

    def copy(src, dst, send, recv, device):
        return pltpu.make_async_remote_copy(
            src_ref=src, dst_ref=dst, send_sem=send, recv_sem=recv,
            device_id=device, device_id_type=MESH,
        )

    barrier = pltpu.get_barrier_semaphore()
    for device in near:
        pl.semaphore_signal(barrier, inc=1, device_id=device, device_id_type=MESH)
    load = pltpu.make_async_copy(white_ref, white_l, load_s)
    load.start()
    table = make_table(orders_ref)
    tab[2 * c] = table[0:8]
    tab[2 * c + 1] = table[8:16]
    pl.semaphore_wait(barrier, len(near))

    def table_copy(j):
        mine = tab.at[pl.ds(2 * c, 2)]
        return copy(mine, mine, table_s.at[j - 1], table_r.at[j - 1], {"coef": (c + 8 - j) % 8, "obs": o})

    for j in range(1, 8):
        table_copy(j).start()
    whites = []
    for n, (block, way) in enumerate([(7, 0), (5, 1), (6, 0), (4, 1), (2, 0), (3, 1), (1, 1), (0, 1)]):
        area = (pl.ds(block * 128, 128), pl.ds(0, (block + 1) * 128))
        whites.append(copy(white_ref.at[area], white_o.at[area], white_s.at[n], white_r.at[n],
                           y_up if way == 0 else y_down))
    for w in whites:
        w.start()
    prepare(index_ref, colat_ref, long_ref, observed_ref, rows_l)
    row_copy = copy(rows_l, rows_o, rows_s, rows_r, y_up)
    row_copy.start()

    for block in range(4):
        white_o[block * TILE:block * TILE + 128, block * TILE + 128:(block + 1) * TILE] = jnp.zeros((128, 128), BF16)
    parity = (lax.broadcasted_iota(jnp.int32, (8, SEG), 0) % 2).astype(F32)

    def triangular(operand, white, put):
        for block in range(SEG // TILE):
            depth = (block + 1) * TILE
            put(block, lax.dot_general(
                operand[:, :depth], white[pl.ds(block * TILE, TILE), pl.ds(0, depth)], NT,
                preferred_element_type=F32))

    def keep_level(level, value):
        for part in range(8):
            dscr[part, pl.ds(level, 8, stride=PITCH), :] = value[:, part * 128:(part + 1) * 128]

    def design(rows, d, dst):
        set_x, set_y = chip_of((here + d) % NSETS)
        coefs = tab[4 * set_x + set_y]
        order, log_const = coefs[:, 0:1], coefs[:, 64:65]
        sectorial = math.sqrt(2.0) * jnp.exp(log_const + order * rows[0:1, :])
        cosine = jnp.broadcast_to(rows[1:2, :], (8, SEG))
        turn = order * rows[2:3, :] - 0.25 * parity
        turn = turn - jnp.floor(turn + 0.5)
        square = turn * turn
        harmonic = jnp.full_like(square, COS_TERMS[-1])
        for term in COS_TERMS[-2::-1]:
            harmonic = harmonic * square + term
        lower = sectorial * harmonic
        lowest = jnp.zeros_like(lower)
        keep_level(0, lower)
        for level in range(1, LEV):
            value = (coefs[:, level:level + 1] * cosine) * lower - coefs[:, 64 + level:65 + level] * lowest
            keep_level(level, value)
            lower, lowest = value, lower
            if level % 8 == 7:
                yield
        for slot in range(8):
            for part in range(8):
                dst[slot * LEV:(slot + 1) * LEV, part * 128:(part + 1) * 128] = (
                    dscr[part, slot * PITCH:slot * PITCH + LEV, :].astype(BF16))
            yield

    def whiten(white, src, dst):
        for block in range(SEG // TILE):
            depth = (block + 1) * TILE
            value = lax.dot_general(
                src[:, :depth], white[block * TILE:(block + 1) * TILE, :depth], NT, preferred_element_type=F32)
            dst[:, block * TILE:(block + 1) * TILE] = value.astype(BF16)

    def make_whitened(rows, white):
        pieces = split_rows(rows[3:4, :])

        def put(block, value):
            row = jnp.sum(value, axis=0, keepdims=True)
            wv[:, block * TILE:(block + 1) * TILE] = split_rows(row)

        triangular(pieces, white, put)

    def rhs_terms(src):
        terms = lax.dot_general(wv[...], src[...], NT, preferred_element_type=F32)
        return jnp.broadcast_to(jnp.sum(terms, axis=0, keepdims=True), (8, SET))

    order_z = [z, 3 - z, 3 - z_odd, z_odd]

    def keep_left(src, column):
        for half, kk in enumerate((1 - k, k)):
            for n, zz in enumerate(order_z):
                left[half * 256 + n * 64:half * 256 + n * 64 + 64, column:column + SEG] = (
                    src[pl.ds(pl.multiple_of((2 * zz + kk) * 64, 64), 64), :])

    def product(n, column, src):
        return lax.dot_general(left[:, column:column + SEG], src[n * 256:(n + 1) * 256, :], NT, preferred_element_type=F32)

    def own_terms(d):
        for n in range(2):
            part[d, :, n * 256:(n + 1) * 256] = product(n, 0, filt)
            yield

    interleave(design(rows_l, 0, dbf))
    load.wait()
    make_whitened(rows_l, white_l)

    def own_stage(d, carry):
        whiten(white_l, dbf, filt)

        @pl.when(d == 0)
        def _():
            keep_left(filt, 0)
            sR[0] = rhs_terms(filt)

        @pl.when(d == 0)
        def _():
            for j in range(1, 8):
                table_copy(j).wait()

        interleave(own_terms(d), design(rows_l, d + 1, dbf))
        return carry

    lax.fori_loop(0, NEAR - 1, own_stage, 0)
    whiten(white_l, dbf, filt)
    row_copy.wait()
    interleave(own_terms(NEAR - 1), in_turn(design(rows_o, 0, dbf0), design(rows_o, set_of(0), dbf)))
    for w in whites:
        w.wait()
    whiten(white_o, dbf0, filt0)
    make_whitened(rows_o, white_o)
    keep_left(filt0, SEG)

    def rhs_copy(n):
        return copy(sR.at[n], rR.at[n], r_s.at[n], r_r.at[n], (sibling, z_first, z_second, y_pair)[n])

    def rhs_step(n):
        rhs_copy(n).wait()
        if n < 3:
            sR[n + 1] = sR[n] + rR[n]
            rhs_copy(n + 1).start()
        else:
            for zz in range(4):
                lanes = slice(zz * 128, (zz + 1) * 128)
                rhs_ref[0:1, pl.ds(pl.multiple_of(zz * 256 + y_lo * 128, 128), 128)] = sR[3, 0:1, lanes]
                rhs_ref[0:1, pl.ds(pl.multiple_of(zz * 256 + (1 - y_lo) * 128, 128), 128)] = rR[3, 0:1, lanes]

    def base_of(q):
        set_x, set_y = chip_of(q)
        return (2 * set_x + set_y // 2) * 1024 + (set_y % 2) * 128

    def k_copy(j):
        return copy(sK.at[j], rK.at[j], k_s.at[j], k_r.at[j], sibling)

    def z_copies(j):
        return [copy(sZ.at[j, h], rZ.at[j, h], z_s.at[j, h], z_r.at[j, h], (z_first, z_second)[h]) for h in range(2)]

    def y_copies(j):
        return [copy(sY.at[j, h], rY.at[j, h], y_s.at[j, h], y_r.at[j, h], (z_second, z_first)[h]) for h in range(2)]

    def t_copy(j, slot):
        q = (here + set_of(j)) % NSETS
        return copy(sT.at[j, slot], rT.at[j, 2 * z + k], t_s.at[j, slot], t_r.at[j],
                    at(*chip_of(q), slot // 2, slot % 2))

    def far_copies():
        return [copy(sD.at[h], rD.at[h], d_s.at[h], d_r.at[h], (z_second, z_far, z_first)[h]) for h in range(3)]

    def emit(total, d):
        base = base_of((here + d) % NSETS)
        for zz in range(4):
            out_ref[:, pl.ds(pl.multiple_of(base + zz * 256, 128), 128)] = total[:, zz * 128:(zz + 1) * 128]

    def mirror(j, total):
        turned = total.T
        for slot in range(8):
            sT[j, slot] = jnp.concatenate(
                [turned[slot * 64:slot * 64 + 32], turned[slot * 64 + 32:slot * 64 + 64]], axis=1).astype(BF16)

        def send(slot, carry):
            t_copy(j, slot).start()
            return carry

        lax.fori_loop(0, 8, send, 0)

    def finish(j):
        for move in y_copies(j):
            move.wait_recv()
        total = (tot[j % 4] + jnp.concatenate([rY[j, 0], rY[j, 1]], axis=1).astype(F32))
        if not isinstance(j, int) or j < MIRROR:
            mirror(j, total)
        emit(total, 0 if isinstance(j, int) and j == 8 else set_of(j))

    def finish_far():
        for move in far_copies():
            move.wait_recv()
        total = keepD[...] + rD[0].astype(F32) + rD[1].astype(F32) + rD[2].astype(F32)
        mirror(6, total)
        emit(total, 1)

    def third_far():
        k_copy(6).wait_recv()
        for h in range(3):
            rows = slice(64 * (h + 1), 64 * (h + 2))
            sD[h] = (own[0, rows, :] + rK[6, rows, :].astype(F32)).astype(BF16)
        for move in far_copies():
            move.start()
        keepD[...] = own[0, 0:64, :] + rK[6, 0:64, :].astype(F32)

    def second(j):
        par = j % 4
        for move in z_copies(j):
            move.wait_recv()
        sY[j, 0] = (keepA[par, 64:128, :] + rZ[j, 0, 0:64, :].astype(F32)).astype(BF16)
        sY[j, 1] = (keepB[par, 64:128, :] + rZ[j, 1, 64:128, :].astype(F32)).astype(BF16)
        for move in y_copies(j):
            move.start()
        tot[par, :, 0:256] = keepA[par, 0:64, :] + rZ[j, 0, 64:128, :].astype(F32)
        tot[par, :, 256:512] = keepB[par, 0:64, :] + rZ[j, 1, 0:64, :].astype(F32)

    def third(j):
        par, now = j % 4, j % 2
        k_copy(j).wait_recv()
        sZ[j, 0] = (own[now, 128:256, 0:256] + rK[j, 128:256, 0:256].astype(F32)).astype(BF16)
        sZ[j, 1] = (own[now, 64:192, 256:512] + rK[j, 64:192, 256:512].astype(F32)).astype(BF16)
        for move in z_copies(j):
            move.start()
        keepA[par] = own[now, 0:128, 0:256] + rK[j, 0:128, 0:256].astype(F32)
        keepB[par, 0:64, :] = own[now, 0:64, 256:512] + rK[j, 0:64, 256:512].astype(F32)
        keepB[par, 64:128, :] = own[now, 192:256, 256:512] + rK[j, 192:256, 256:512].astype(F32)

    def gram(j, d, src):
        for n in range(2):
            lanes = slice(n * 256, (n + 1) * 256)
            total = part[d, :, lanes] + product(n, SEG, src)
            sK[j, :, lanes] = total[0:256].astype(BF16)
            own[j % 2, :, lanes] = total[256:512]
            yield

    def mirrored(j, carry):
        copy(sT.at[j], rT.at[j], t_s.at[j, 0], t_r.at[j], sibling).wait_recv()
        base = base_of((here + NSETS - set_of(j)) % NSETS)
        for zz in range(4):
            for half in range(2):
                lanes = slice(half * 64, half * 64 + 64)
                piece = jnp.concatenate(
                    [rT[j, 2 * zz, :, lanes].astype(F32), rT[j, 2 * zz + 1, :, lanes].astype(F32)], axis=1)
                out_ref[half * 32:half * 32 + 32, pl.ds(pl.multiple_of(base + zz * 256, 128), 128)] = piece

        def sent(slot, inner):
            t_copy(j, slot).wait_send()
            return inner

        lax.fori_loop(0, 8, sent, 0)
        return carry

    sR[0] = sR[0] + rhs_terms(filt0)
    rhs_copy(0).start()

    def stage(i, carry):
        @pl.when(i >= 2)
        def _():
            third(i - 2)

        for n in range(4):
            @pl.when(i == 2 * n + 1)
            def _(n=n):
                rhs_step(n)

        @pl.when(i >= 7)
        def _():
            finish(i - 7)

        whiten(white_o, dbf, filt)

        @pl.when(i >= 4)
        def _():
            second(i - 4)

        interleave(gram(i, set_of(i), filt), design(rows_o, set_of(jnp.minimum(i + 1, 7)), dbf))
        k_copy(i).start()
        return carry

    lax.fori_loop(0, 8, stage, 0)
    third_far()
    finish(1)
    interleave(gram(8, 0, filt0))
    k_copy(8).start()
    second(4)
    third(7)
    finish(2)
    third(8)
    second(5)
    finish(3)
    finish_far()
    finish(4)
    second(7)
    lax.fori_loop(0, 1, mirrored, 0)
    finish(5)
    second(8)
    lax.fori_loop(1, 3, mirrored, 0)
    finish(7)
    lax.fori_loop(3, 4, mirrored, 0)
    finish(8)
    lax.fori_loop(4, MIRROR, mirrored, 0)

    def drain(j, carry):
        k_copy(j).wait_send()
        return carry

    lax.fori_loop(0, NEAR, drain, 0)

    def drain_z(j, carry):
        for move in z_copies(j) + y_copies(j):
            move.wait_send()
        return carry

    lax.fori_loop(0, 6, drain_z, 0)
    lax.fori_loop(7, 9, drain_z, 0)
    for move in far_copies():
        move.wait_send()


def on_device(sample_index, colatitude, longitude, orders, observed, whitening):
    vmem = pl.BlockSpec(memory_space=pltpu.VMEM)
    V = pltpu.VMEM
    dma = pltpu.SemaphoreType.DMA
    normal, rhs = pl.pallas_call(
        main_kernel,
        out_shape=(jax.ShapeDtypeStruct((64, 8192), F32), jax.ShapeDtypeStruct((1, SEG), F32)),
        in_specs=[vmem] * 5 + [pl.BlockSpec(memory_space=pl.ANY)],
        out_specs=(vmem, vmem),
        scratch_shapes=[
            V((NSETS, 8, 128), F32), V((8, SEG), F32), V((8, SEG), F32),
            V((SEG, SEG), BF16), V((SEG, SEG), BF16),
            V((8, 8 * PITCH, 128), F32), V((SET, SEG), BF16), V((SET, SEG), BF16), V((SET, SEG), BF16), V((SET, SEG), BF16),
            V((NEAR, SET, SET), F32),
            V((SET, 2 * SEG), BF16), V((16, SEG), BF16), V((2, 256, SET), F32),
            V((NEAR, 256, SET), BF16), V((NEAR, 256, SET), BF16),
            V((NEAR, 2, 128, 256), BF16), V((NEAR, 2, 128, 256), BF16),
            V((NEAR, 2, 64, 256), BF16), V((NEAR, 2, 64, 256), BF16),
            V((4, 128, 256), F32), V((4, 128, 256), F32), V((64, SET), F32), V((4, 64, SET), F32),
            V((3, 64, SET), BF16), V((3, 64, SET), BF16),
            V((MIRROR, 8, 32, 128), BF16), V((MIRROR, 8, 32, 128), BF16),
            V((4, 8, SET), F32), V((4, 8, SET), F32),
            dma, dma((7,)), dma((7,)), dma, dma, dma((8,)), dma((8,)),
            dma((NEAR,)), dma((NEAR,)), dma((NEAR, 2)), dma((NEAR, 2)),
            dma((NEAR, 2)), dma((NEAR, 2)), dma((3,)), dma((3,)), dma((MIRROR, 8)), dma((MIRROR,)),
            dma((4,)), dma((4,)),
        ],
        compiler_params=pltpu.CompilerParams(
            collective_id=0, has_side_effects=True, vmem_limit_bytes=60 * 2**20,
        ),
    )(
        sample_index.reshape(1, SEG), colatitude.reshape(128, 128), longitude.reshape(128, 128),
        orders.reshape(1, 16), observed.reshape(1, SEG), whitening,
    )
    rows = 16.0 * SEG
    return normal * (1.0 / rows), rhs.reshape(SEG) * (1.0 / math.sqrt(rows))


def solution(mesh):
    placed = (P("obs"), P(), P(), P("coef"), P("obs"), P("obs", None))
    return jax.shard_map(
        on_device,
        mesh=mesh,
        in_specs=placed,
        out_specs=(P(("coef", "obs"), None), P("coef")),
        check_vma=False,
    )
```

time: 144 us -> 74.9 us (0.52)
  Pallas kernels: 142 us -> 70.4 us
  other arithmetic: 0 us -> 3.66 us
    pallas_call x1 -> x0, Pallas kernels: 65.9 us -> none  [on_device(): pl.pallas_call(hand_over, out_shape=(jax.ShapeDtypeStruct((64, 8192), F32...]
    pallas_call x1, Pallas kernels: 76.1 us -> 70.4 us  [on_device(): pl.pallas_call(main_kernel, out_shape=(jax.ShapeDtypeStruct((64, 8192), F...]
    mul x0 -> x2, other arithmetic: none -> 3.66 us  [on_device(): return (normal * (1.0 / rows), rhs.reshape(SEG) * (1.0 / math.sqrt(rows)))]
where the time goes in v4:
time: 74.9 us; the launch traced here: 74.7 us
  Pallas kernels  70.4 us (94%)
  other arithmetic  3.66 us (5%)
    pallas_call x1, Pallas kernels, on_device(): pl.pallas_call(main_kernel, out_shape=(jax.ShapeDtypeStruct((64, 8192), F...  70.4 us
    mul x2, other arithmetic, on_device(): return (normal * (1.0 / rows), rhs.reshape(SEG) * (1.0 / math.sqrt(rows)))  3.66 us

profile of v4, /device:TPU:1, one launch (start us, length us, event | category | flops | bytes accessed | tf_op | source)
XLA Modules:
  0.0 74.7 jit_solution(14679057917123030757)
XLA Ops:
  0.6 70.4 %shard_map.77 = (f32[64,8192]{1,0:T(8,128)}, f32[1,1024]{1,0:T(1,128)}) custom-call(s32[1,1024]{1,0:T(1,128)} %bitcast.8, f32[128,128]{1,0:T(8,128)} %bitcast.6, f32[128,128]{1,0:T(8,128)} %bitcast.7, s32[1,16]{1,0:T(1,128)} %bitcast.11, f32[1,1024]{1,0:T(1,128)} %bitcast.9, bf16[1024,1024]{1,0:T(8,128)(2,1)} %white_ref.1), custom_call_target="tpu_custom_call" | custom-call | tf_op jit(solution)/shard_map/pallas_call | solution.py:470
  71.1 0.0 copy-start
  71.1 3.1 %broadcast_multiply_fusion = f32[64,8192]{1,0:T(8,128)} fusion(f32[64,8192]{1,0:T(8,128)} %get-tuple-element.4), kind=kLoop, calls=%fused_computation | loop fusion | flops 524288 | bytes 4194304 | tf_op jit(solution)/shard_map/mul | solution.py:501
  74.1 0.0 copy-done
  74.1 0.6 broadcast_multiply_fusion.1
Async XLA Ops:
  71.1 3.1 %copy-start = (f32[1,1024]{1,0:T(1,128)S(1)}, f32[1,1024]{1,0:T(1,128)}, u32[]{:S(2)}) copy-start(f32[1,1024]{1,0:T(1,128)} %get-tuple-element.5) | copy-start | bytes 12292

commit v5 on v4

--- a/solution.py
+++ b/solution.py
@@ -107,9 +107,9 @@
 def main_kernel(
     index_ref, colat_ref, long_ref, orders_ref, observed_ref, white_ref, out_ref, rhs_ref,
     tab, rows_l, rows_o, white_l, white_o, dscr, dbf, dbf0, filt, filt0, part, left, wv, own,
-    sK, rK, sZ, rZ, sY, rY, keepA, keepB, keepD, tot, sD, rD, sT, rT, sR, rR,
+    sK, rK, sZ, rZ, sY, rY, keepA, keepB, tot, sT, rT, sR, rR,
     load_s, table_s, table_r, rows_s, rows_r, white_s, white_r,
-    k_s, k_r, z_s, z_r, y_s, y_r, d_s, d_r, t_s, t_r, r_s, r_r,
+    k_s, k_r, z_s, z_r, y_s, y_r, t_s, t_r, r_s, r_r,
 ):
     c, o = lax.axis_index("coef"), lax.axis_index("obs")
     x, y_hi = c // 2, c % 2
@@ -128,8 +128,7 @@
     y_up = at(x, (y + 1) % 4, z, k)
     y_down = at(x, (y + 3) % 4, z, k)
     y_pair = at(x, y + 1 - 2 * y_lo, z, k)
-    z_far = at(x, y, (z + 2) % 4, k)
-    near = [sibling, z_first, z_second, z_far, y_up, y_down]
+    near = [sibling, z_first, z_second, y_up, y_down]
     near += [{"coef": (c + j) % 8, "obs": o} for j in range(1, 8)]
 
     def copy(src, dst, send, recv, device):
@@ -305,9 +304,6 @@
         return copy(sT.at[j, slot], rT.at[j, 2 * z + k], t_s.at[j, slot], t_r.at[j],
                     at(*chip_of(q), slot // 2, slot % 2))
 
-    def far_copies():
-        return [copy(sD.at[h], rD.at[h], d_s.at[h], d_r.at[h], (z_second, z_far, z_first)[h]) for h in range(3)]
-
     def emit(total, d):
         base = base_of((here + d) % NSETS)
         for zz in range(4):
@@ -332,22 +328,6 @@
         if not isinstance(j, int) or j < MIRROR:
             mirror(j, total)
         emit(total, 0 if isinstance(j, int) and j == 8 else set_of(j))
-
-    def finish_far():
-        for move in far_copies():
-            move.wait_recv()
-        total = keepD[...] + rD[0].astype(F32) + rD[1].astype(F32) + rD[2].astype(F32)
-        mirror(6, total)
-        emit(total, 1)
-
-    def third_far():
-        k_copy(6).wait_recv()
-        for h in range(3):
-            rows = slice(64 * (h + 1), 64 * (h + 2))
-            sD[h] = (own[0, rows, :] + rK[6, rows, :].astype(F32)).astype(BF16)
-        for move in far_copies():
-            move.start()
-        keepD[...] = own[0, 0:64, :] + rK[6, 0:64, :].astype(F32)
 
     def second(j):
         par = j % 4
@@ -424,7 +404,7 @@
         return carry
 
     lax.fori_loop(0, 8, stage, 0)
-    third_far()
+    third(6)
     finish(1)
     interleave(gram(8, 0, filt0))
     k_copy(8).start()
@@ -434,12 +414,13 @@
     third(8)
     second(5)
     finish(3)
-    finish_far()
+    second(6)
     finish(4)
     second(7)
+    finish(5)
     lax.fori_loop(0, 1, mirrored, 0)
-    finish(5)
     second(8)
+    finish(6)
     lax.fori_loop(1, 3, mirrored, 0)
     finish(7)
     lax.fori_loop(3, 4, mirrored, 0)
@@ -457,10 +438,7 @@
             move.wait_send()
         return carry
 
-    lax.fori_loop(0, 6, drain_z, 0)
-    lax.fori_loop(7, 9, drain_z, 0)
-    for move in far_copies():
-        move.wait_send()
+    lax.fori_loop(0, NEAR, drain_z, 0)
 
 
 def on_device(sample_index, colatitude, longitude, orders, observed, whitening):
@@ -481,13 +459,12 @@
             V((NEAR, 256, SET), BF16), V((NEAR, 256, SET), BF16),
             V((NEAR, 2, 128, 256), BF16), V((NEAR, 2, 128, 256), BF16),
             V((NEAR, 2, 64, 256), BF16), V((NEAR, 2, 64, 256), BF16),
-            V((4, 128, 256), F32), V((4, 128, 256), F32), V((64, SET), F32), V((4, 64, SET), F32),
-            V((3, 64, SET), BF16), V((3, 64, SET), BF16),
+            V((4, 128, 256), F32), V((4, 128, 256), F32), V((4, 64, SET), F32),
             V((MIRROR, 8, 32, 128), BF16), V((MIRROR, 8, 32, 128), BF16),
             V((4, 8, SET), F32), V((4, 8, SET), F32),
             dma, dma((7,)), dma((7,)), dma, dma, dma((8,)), dma((8,)),
             dma((NEAR,)), dma((NEAR,)), dma((NEAR, 2)), dma((NEAR, 2)),
-            dma((NEAR, 2)), dma((NEAR, 2)), dma((3,)), dma((3,)), dma((MIRROR, 8)), dma((MIRROR,)),
+            dma((NEAR, 2)), dma((NEAR, 2)), dma((MIRROR, 8)), dma((MIRROR,)),
             dma((4,)), dma((4,)),
         ],
         compiler_params=pltpu.CompilerParams(

time: 74.9 us -> 73.8 us (0.985)
  Pallas kernels: 70.4 us -> 69.1 us
    pallas_call x1, Pallas kernels: 70.4 us -> 69.1 us  [on_device(): pl.pallas_call(main_kernel, out_shape=(jax.ShapeDtypeStruct((64, 8192), F...]
where the time goes in v5:
time: 73.8 us; the launch traced here: 73.4 us
  Pallas kernels  69.1 us (94%)
  other arithmetic  3.66 us (5%)
    pallas_call x1, Pallas kernels, on_device(): pl.pallas_call(main_kernel, out_shape=(jax.ShapeDtypeStruct((64, 8192), F...  69.1 us
    mul x2, other arithmetic, on_device(): return (normal * (1.0 / rows), rhs.reshape(SEG) * (1.0 / math.sqrt(rows)))  3.66 us

profile of v5, /device:TPU:1, one launch (start us, length us, event | category | flops | bytes accessed | tf_op | source)
XLA Modules:
  0.0 73.4 jit_solution(10217284958673296701)
XLA Ops:
  0.6 69.1 %shard_map.77 = (f32[64,8192]{1,0:T(8,128)}, f32[1,1024]{1,0:T(1,128)}) custom-call(s32[1,1024]{1,0:T(1,128)} %bitcast.8, f32[128,128]{1,0:T(8,128)} %bitcast.6, f32[128,128]{1,0:T(8,128)} %bitcast.7, s32[1,16]{1,0:T(1,128)} %bitcast.11, f32[1,1024]{1,0:T(1,128)} %bitcast.9, bf16[1024,1024]{1,0:T(8,128)(2,1)} %white_ref.1), custom_call_target="tpu_custom_call" | custom-call | tf_op jit(solution)/shard_map/pallas_call | solution.py:448
  69.7 0.0 copy-start
  69.7 3.1 %broadcast_multiply_fusion = f32[64,8192]{1,0:T(8,128)} fusion(f32[64,8192]{1,0:T(8,128)} %get-tuple-element.4), kind=kLoop, calls=%fused_computation | loop fusion | flops 524288 | bytes 4194304 | tf_op jit(solution)/shard_map/mul | solution.py:478
  72.8 0.0 copy-done
  72.8 0.6 broadcast_multiply_fusion.1
Async XLA Ops:
  69.7 3.1 %copy-start = (f32[1,1024]{1,0:T(1,128)S(1)}, f32[1,1024]{1,0:T(1,128)}, u32[]{:S(2)}) copy-start(f32[1,1024]{1,0:T(1,128)} %get-tuple-element.5) | copy-start | bytes 12292

commit v6 on v5

--- a/solution.py
+++ b/solution.py
@@ -384,20 +384,24 @@
         def _():
             third(i - 2)
 
-        for n in range(4):
+        for n in range(3):
             @pl.when(i == 2 * n + 1)
             def _(n=n):
                 rhs_step(n)
 
-        @pl.when(i >= 7)
-        def _():
-            finish(i - 7)
-
         whiten(white_o, dbf, filt)
 
         @pl.when(i >= 4)
         def _():
             second(i - 4)
+
+        @pl.when(i == 6)
+        def _():
+            rhs_step(3)
+
+        @pl.when(i >= 6)
+        def _():
+            finish(i - 6)
 
         interleave(gram(i, set_of(i), filt), design(rows_o, set_of(jnp.minimum(i + 1, 7)), dbf))
         k_copy(i).start()
@@ -405,11 +409,10 @@
 
     lax.fori_loop(0, 8, stage, 0)
     third(6)
-    finish(1)
     interleave(gram(8, 0, filt0))
     k_copy(8).start()
+    third(7)
     second(4)
-    third(7)
     finish(2)
     third(8)
     second(5)
@@ -453,7 +456,7 @@
         scratch_shapes=[
             V((NSETS, 8, 128), F32), V((8, SEG), F32), V((8, SEG), F32),
             V((SEG, SEG), BF16), V((SEG, SEG), BF16),
-            V((8, 8 * PITCH, 128), F32), V((SET, SEG), BF16), V((SET, SEG), BF16), V((SET, SEG), BF16), V((SET, SEG), BF16),
+            V((8, 9 * PITCH + 7, 128), F32), V((SET, SEG), BF16), V((SET, SEG), BF16), V((SET, SEG), BF16), V((SET, SEG), BF16),
             V((NEAR, SET, SET), F32),
             V((SET, 2 * SEG), BF16), V((16, SEG), BF16), V((2, 256, SET), F32),
             V((NEAR, 256, SET), BF16), V((NEAR, 256, SET), BF16),

time: 73.8 us -> 73.1 us (level)
  no operation moved by 1% of the time
where the time goes in v6:
time: 73.1 us; the launch traced here: 72.9 us
  Pallas kernels  68.6 us (94%)
  other arithmetic  3.66 us (5%)
    pallas_call x1, Pallas kernels, on_device(): pl.pallas_call(main_kernel, out_shape=(jax.ShapeDtypeStruct((64, 8192), F...  68.6 us
    mul x2, other arithmetic, on_device(): return (normal * (1.0 / rows), rhs.reshape(SEG) * (1.0 / math.sqrt(rows)))  3.66 us

profile of v6, /device:TPU:1, one launch (start us, length us, event | category | flops | bytes accessed | tf_op | source)
XLA Modules:
  0.0 72.9 jit_solution(8982284932806438508)
XLA Ops:
  0.6 68.6 %shard_map.77 = (f32[64,8192]{1,0:T(8,128)}, f32[1,1024]{1,0:T(1,128)}) custom-call(s32[1,1024]{1,0:T(1,128)} %bitcast.8, f32[128,128]{1,0:T(8,128)} %bitcast.6, f32[128,128]{1,0:T(8,128)} %bitcast.7, s32[1,16]{1,0:T(1,128)} %bitcast.11, f32[1,1024]{1,0:T(1,128)} %bitcast.9, bf16[1024,1024]{1,0:T(8,128)(2,1)} %white_ref.1), custom_call_target="tpu_custom_call" | custom-call | tf_op jit(solution)/shard_map/pallas_call | solution.py:451
  69.3 0.0 copy-start
  69.3 3.1 %broadcast_multiply_fusion = f32[64,8192]{1,0:T(8,128)} fusion(f32[64,8192]{1,0:T(8,128)} %get-tuple-element.4), kind=kLoop, calls=%fused_computation | loop fusion | flops 524288 | bytes 4194304 | tf_op jit(solution)/shard_map/mul | solution.py:481
  72.3 0.0 copy-done
  72.3 0.6 broadcast_multiply_fusion.1
Async XLA Ops:
  69.3 3.1 %copy-start = (f32[1,1024]{1,0:T(1,128)S(1)}, f32[1,1024]{1,0:T(1,128)}, u32[]{:S(2)}) copy-start(f32[1,1024]{1,0:T(1,128)} %get-tuple-element.5) | copy-start | bytes 12292
